TPU v7x, 32 devices: a whole 2x2x4 slice. The times are simulated.
32 devices in a mesh: seq: 4 (over z), mp: 4 (over y, core), dp: 2 (over x).
Axes of the slice: x: 2, y: 2, z: 4, core: 2. Of those that a mesh axis runs over, the one named last changes fastest.
Arguments:
- residual_in: bfloat16 [3072, 2048], P(('dp', 'seq')), parts along dimension 0, may hold values from -6 to 6
- queries: bfloat16 [3072, 2048], P(('dp', 'seq'), 'mp'), parts along dimension 0, may hold values from -30 to 30
- keys: bfloat16 [3072, 2048], P(('dp', 'seq'), 'mp'), parts along dimension 0, may hold values from -10 to 10
- values: bfloat16 [3072, 2048], P(('dp', 'seq'), 'mp'), parts along dimension 0, may hold values from -6 to 6
- w_out: bfloat16 [2048, 2048], P('mp', 'seq'), may hold values from -0.1875 to 0.1875
- conv_value: bfloat16 [2048, 2048], P('seq', 'mp'), may hold values from -0.125 to 0.125
- conv_gate: bfloat16 [2048, 2048], P('seq', 'mp'), may hold values from -0.125 to 0.125
- depth_kernel: float32 [31, 2048], P(None, 'mp'), may hold values from -2 to 2
- conv_out: bfloat16 [2048, 2048], P('mp', 'seq'), may hold values from -0.25 to 0.25
- ffn_in: bfloat16 [2048, 8192], P('seq', 'mp'), may hold values from -0.125 to 0.125
- ffn_down: bfloat16 [8192, 2048], P('mp', 'seq'), may hold values from -0.1875 to 0.1875
- ffn_mask: int32 [24, 64], P(('dp', 'seq'), 'mp'), parts along dimension 0, may hold values 0 or 1
Outputs:
- block_out: float32 [3072, 2048], P(('dp', 'seq', 'mp')), parts along dimension 0
There are 2 independent parts, one for each index of `dp`. A program takes and returns all parts, laid end to end along the dimension named above; an argument that names none is the same for every part. Nothing has to cross between parts.
All inputs are finite; a program needn't handle non-finite values. No bound on the sum of `ffn_mask` on one device may be relied on, other than what follows from the above.
Results may differ from a plain program's by a relative error of at most 0.017.
Values may be sent and summed in bfloat16 or wider, within the bound.
No kernel may reach another device: no remote copies, remote signals or barrier semaphores. Data moves between devices by JAX's collectives and lax.ppermute only.
A program may use at most 128 MiB of HBM per device.

v0:
```python
import functools
import math

import jax
import jax.numpy as jnp
from jax import lax
from jax.experimental import pallas as pl
from jax.experimental.pallas import tpu as pltpu
from jax.sharding import PartitionSpec as P

HEAD_DIM = 128


norm_epsilon = 1e-05


def ring_pairs(axis):
    count = lax.axis_size(axis)
    return [(i, (i + 1) % count) for i in range(count)]


class Line:
    def __init__(self, depth):
        self.depth, self.waiting, self.under_way, self.crossing = depth, [], [], []
        self.parts = {}

    def add(self, weights):
        for t in range(1, lax.axis_size("seq")):
            for name, array, dim in weights:
                self.waiting.append((name, t, dim))
                if t == 1:
                    self.parts[name, 0] = own_parts(array, dim)

    def start(self):
        if not self.waiting:
            return
        name, t, dim = self.waiting[0]
        if (name, t - 1) not in self.parts:
            return
        del self.waiting[0]
        piece = self.parts[name, t - 1][0]
        if self.token is not None:
            piece, _ = lax.optimization_barrier((piece, self.token))
        self.under_way.append((name, t, dim, lax.ppermute(piece, "seq", ring_pairs("seq"))))

    def begin(self):
        self.token = None
        while len(self.under_way) < self.depth:
            self.start()

    def visit(self, *beside):
        crossed = None
        if self.under_way:
            name, t, dim, piece = self.under_way.pop(0)
            if len(self.crossing) > 1:
                crossed = self.crossing.pop(0)
                (beside, piece, taken) = lax.optimization_barrier((beside, piece, crossed[2]))
            else:
                (beside, piece) = lax.optimization_barrier((beside, piece))
            self.token = piece
            parts = [piece]
            self.parts[name, t] = parts
            while len(self.under_way) < self.depth:
                held = len(self.under_way)
                self.start()
                if len(self.under_way) == held:
                    break
            if dim is not None:
                for _ in range(1, lax.axis_size("dp")):
                    piece = lax.ppermute(piece, "dp", ring_pairs("dp"))
                    self.crossing.append((name, t, piece))
        elif self.crossing:
            crossed = self.crossing.pop(0)
            (beside, taken) = lax.optimization_barrier((beside, crossed[2]))
        if crossed is not None:
            self.parts[crossed[0], crossed[1]].append(taken)
        return beside if len(beside) != 1 else beside[0]

    def visits(self, number, beside):
        for _ in range(number * (lax.axis_size("seq") - 1) // 3):
            beside = self.visit(beside)
        return beside

    def has(self, name, first=0, last=None):
        last = lax.axis_size("seq") if last is None else last
        width = len(self.parts[name, 0])
        return all(len(self.parts.get((name, t), ())) == width for t in range(first, last))

    def until(self, names, beside, first=0, last=None):
        while not all(self.has(name, first, last) for name in names):
            beside = self.visit(beside)
        return beside

    def take(self, name, dim, first=0, last=None):
        last = lax.axis_size("seq") if last is None else last
        parts = [part for t in range(first, last) for part in self.parts[name, t]]
        if parts[0].shape[dim] % 128:
            parts = [jnp.concatenate(parts, axis=dim)]
        return parts


def part_of(weight, dim, index):
    width = weight.shape[dim] // lax.axis_size("dp")
    return lax.dynamic_slice_in_dim(weight, index * width, width, axis=dim)


def own_parts(array, dim):
    if dim is None:
        return [array]
    count, here = lax.axis_size("dp"), lax.axis_index("dp")
    return [part_of(array, dim, (here - p) % count) for p in range(count)]


def to_held_order(value):
    count, part_count = lax.axis_size("seq"), lax.axis_size("dp")
    s, h = lax.axis_index("seq"), lax.axis_index("dp")
    width = value.shape[1] // (count * part_count)
    return jnp.concatenate(
        [
            lax.dynamic_slice_in_dim(
                value, ((s - t) % count * part_count + (h - p) % part_count) * width, width, axis=1
            )
            for t in range(count)
            for p in range(part_count)
        ],
        axis=1,
    )


def to_natural_order(value):
    count, part_count = lax.axis_size("seq"), lax.axis_size("dp")
    s, h = lax.axis_index("seq"), lax.axis_index("dp")
    width = value.shape[1] // (count * part_count)
    return jnp.concatenate(
        [
            lax.dynamic_slice_in_dim(
                value, ((s - b) % count * part_count + (h - q) % part_count) * width, width, axis=1
            )
            for b in range(count)
            for q in range(part_count)
        ],
        axis=1,
    )


def layer_norm(stream):
    row_mean = jnp.mean(stream, axis=-1, keepdims=True)
    centered = stream - row_mean
    spread_of = jnp.mean(centered * centered, axis=-1, keepdims=True)
    return centered * lax.rsqrt(spread_of + norm_epsilon)


def dot(left, right):
    return jnp.dot(left, right, preferred_element_type=jnp.float32)


def xor_pairs(count, bit):
    return [(i, i ^ bit) for i in range(count)]


def scatter_sum(sent, kept, line, visits):
    count = lax.axis_size("mp")
    me = lax.axis_index("mp")
    bit = 1
    while True:
        taken = lax.ppermute(sent, "mp", xor_pairs(count, bit))
        kept = line.visits(visits[0] if bit == 1 else visits[1], kept)
        part = kept + taken.astype(jnp.float32)
        bit *= 2
        if bit == count:
            return part[0]
        groups = part.reshape(-1, 2, *part.shape[1:])
        mine = (me // bit) % 2
        sent = lax.dynamic_index_in_dim(groups, 1 - mine, 1, keepdims=False).astype(jnp.bfloat16)
        kept = lax.dynamic_index_in_dim(groups, mine, 1, keepdims=False)


def widen(rows, line, visits):
    count = lax.axis_size("mp")
    me = lax.axis_index("mp")
    share, width = rows.shape
    bit = count // 2
    held = rows[None]
    while bit:
        taken = lax.ppermute(held, "mp", xor_pairs(count, bit))
        held = line.visits(visits[1] if bit > 1 else visits[0], held)
        first = (me // bit) % 2 == 0
        held = jnp.stack(
            [jnp.where(first, held, taken), jnp.where(first, taken, held)], axis=1
        ).reshape(-1, share, width)
        bit //= 2
    return held.reshape(count * share, width)


def kernel_call(kernel, outs, args, scratch=(), scalars=0):
    return pl.pallas_call(
        kernel,
        out_shape=outs,
        in_specs=[pl.BlockSpec(memory_space=pltpu.SMEM)] * scalars
        + [pl.BlockSpec(memory_space=pltpu.VMEM)] * (len(args) - scalars),
        out_specs=jax.tree.map(lambda _: pl.BlockSpec(memory_space=pltpu.VMEM), outs),
        scratch_shapes=scratch,
        compiler_params=pltpu.CompilerParams(vmem_limit_bytes=56 * 1024 * 1024),
    )(*args)


def attention_kernel(count, q_ref, *refs):
    k_refs, v_refs, o_ref = refs[:count], refs[count : 2 * count], refs[2 * count]
    rows, width = q_ref.shape
    block = 128 if rows % 128 == 0 else rows
    scale = 1.0 / math.sqrt(HEAD_DIM)

    @pl.loop(0, rows // block)
    def _(r):
        here = pl.ds(pl.multiple_of(r * block, block), block)
        for first in range(0, width, HEAD_DIM):
            columns = slice(first, first + HEAD_DIM)
            q = q_ref[here, columns]
            scores = [
                lax.dot_general(
                    q,
                    k_ref[:, columns],
                    (((1,), (1,)), ((), ())),
                    preferred_element_type=jnp.float32,
                )
                * scale
                for k_ref in k_refs
            ]
            top = functools.reduce(
                jnp.maximum, [jnp.max(s, axis=1, keepdims=True) for s in scores]
            )
            weights = [jnp.exp(s - top) for s in scores]
            total = sum(jnp.sum(w, axis=1, keepdims=True) for w in weights)
            mixed = sum(
                dot(w.astype(jnp.bfloat16), v_ref[:, columns])
                for w, v_ref in zip(weights, v_refs)
            )
            o_ref[here, columns] = (mixed / total).astype(o_ref.dtype)


def attention(queries, key_pieces, value_pieces):
    return kernel_call(
        functools.partial(attention_kernel, len(key_pieces)),
        jax.ShapeDtypeStruct(queries.shape, jnp.bfloat16),
        (queries, *key_pieces, *value_pieces),
    )


def share_out(product_ref, sent_ref, kept_ref, columns):
    half, share = sent_ref.shape[:2]
    mine = lax.axis_index("mp") % 2
    for j in range(half):
        theirs = pl.ds(pl.multiple_of((2 * j + 1 - mine) * share, share), share)
        ours = pl.ds(pl.multiple_of((2 * j + mine) * share, share), share)
        sent_ref[j, :, columns] = product_ref[theirs, :].astype(sent_ref.dtype)
        kept_ref[j, :, columns] = product_ref[ours, :]


def project_refs(lefts, parts, sent_ref, kept_ref, product_ref):
    width = product_ref.shape[1]
    for i, blocks in enumerate(parts):
        product_ref[...] = sum(dot(left[...], block[...]) for left, block in zip(lefts, blocks))
        share_out(product_ref, sent_ref, kept_ref, slice(i * width, (i + 1) * width))


def project_kernel(left_count, *refs):
    lefts, (sent_ref, kept_ref, product_ref) = refs[:left_count], refs[-3:]
    blocks = refs[left_count:-3]
    number = len(blocks) // left_count
    project_refs(
        lefts,
        [blocks[i::number] for i in range(number)],
        sent_ref,
        kept_ref,
        product_ref,
    )


def shares(rows, columns):
    count = lax.axis_size("mp")
    shape = (count // 2, rows // count, columns)
    return (
        jax.ShapeDtypeStruct(shape, jnp.bfloat16),
        jax.ShapeDtypeStruct(shape, jnp.float32),
    )


def project(lefts, parts):
    rows, width = lefts[0].shape[0], parts[0][0].shape[1]
    return kernel_call(
        functools.partial(project_kernel, len(lefts)),
        shares(rows, width * len(parts[0])),
        (*lefts, *[block for blocks in parts for block in blocks]),
        [pltpu.VMEM((rows, width), jnp.float32)],
    )


def through(x_ref, parts, columns):
    width = parts[0].shape[0]
    return sum(
        dot(x_ref[:, i * width : (i + 1) * width], part[:, columns])
        for i, part in enumerate(parts)
    )


def column_tiles(width):
    tile = 256 if width % 256 == 0 else width
    return width // tile, tile


def gated_kernel(count, x_ref, *refs):
    value_refs, gate_refs, o_ref = refs[:count], refs[count : 2 * count], refs[2 * count]
    tiles, tile = column_tiles(o_ref.shape[1])

    @pl.loop(0, tiles)
    def _(n):
        columns = pl.ds(pl.multiple_of(n * tile, tile), tile)
        gate = through(x_ref, gate_refs, columns)
        value = through(x_ref, value_refs, columns)
        o_ref[:, columns] = (value / (1.0 + jnp.exp(-gate))).astype(o_ref.dtype)


def gated(normed, value_parts, gate_parts):
    return kernel_call(
        functools.partial(gated_kernel, len(value_parts)),
        jax.ShapeDtypeStruct((normed.shape[0], value_parts[0].shape[1]), jnp.bfloat16),
        (normed, *value_parts, *gate_parts),
    )


def conv_kernel(x_ref, before_ref, after_ref, taps_ref, *refs):
    parts, (sent_ref, kept_ref, product_ref, padded_ref, active_ref) = refs[:-5], refs[-5:]
    edge, rows = before_ref.shape[0], x_ref.shape[0]
    taps = taps_ref.shape[0]
    shift = edge - taps // 2
    padded_ref[:edge, :] = before_ref[...].astype(jnp.float32)
    padded_ref[edge : edge + rows, :] = x_ref[...].astype(jnp.float32)
    padded_ref[edge + rows :, :] = after_ref[...].astype(jnp.float32)
    block = 64 if rows % 64 == 0 else rows
    for first in range(0, x_ref.shape[1], 128):
        columns = slice(first, first + 128)

        @pl.loop(0, rows // block)
        def _(r):
            base = pl.multiple_of(r * block, block)
            window = padded_ref[pl.ds(base, block + 2 * edge), columns]
            total = jnp.zeros((block, window.shape[1]), jnp.float32)
            for t in range(taps):
                total += taps_ref[t : t + 1, columns] * window[t + shift : t + shift + block]
            active_ref[pl.ds(base, block), columns] = (total / (1.0 + jnp.exp(-total))).astype(
                jnp.bfloat16
            )

    project_refs([active_ref], [[part] for part in parts], sent_ref, kept_ref, product_ref)


def conv_branch(units, taps, parts):
    rows, channels = units.shape
    edge = -(-(taps.shape[0] // 2) // 16) * 16
    count = lax.axis_size("seq")
    up = [(i, i + 1) for i in range(count - 1)]
    down = [(j, i) for i, j in up]
    before = lax.ppermute(units[rows - edge :], "seq", up)
    after = lax.ppermute(units[:edge], "seq", down)
    width = parts[0].shape[1]
    return kernel_call(
        conv_kernel,
        shares(rows, width * len(parts)),
        (units, before, after, taps, *parts),
        [
            pltpu.VMEM((rows, width), jnp.float32),
            pltpu.VMEM((rows + 2 * edge, channels), jnp.float32),
            pltpu.VMEM((rows, channels), jnp.bfloat16),
        ],
    )


def hidden_kernel(mask_ref, x_ref, *refs):
    parts, o_ref = refs[:-1], refs[-1]
    rows, width = o_ref.shape
    tile_rows, block = rows // mask_ref.shape[0], width // mask_ref.shape[1]
    tiles, tile = column_tiles(width)

    @pl.loop(0, tiles)
    def _(n):
        units = through(x_ref, parts, pl.ds(pl.multiple_of(n * tile, tile), tile))
        units = units / (1.0 + jnp.exp(-units))
        for r in range(mask_ref.shape[0]):
            for j in range(tile // block):
                factor = mask_ref[r, n * (tile // block) + j].astype(jnp.float32)
                masked = (
                    units[r * tile_rows : (r + 1) * tile_rows, j * block : (j + 1) * block] * factor
                )
                o_ref[
                    r * tile_rows : (r + 1) * tile_rows,
                    pl.ds(pl.multiple_of(n * tile + j * block, block), block),
                ] = masked.astype(o_ref.dtype)


def hidden_of(normed, parts, mask):
    return kernel_call(
        hidden_kernel,
        jax.ShapeDtypeStruct((normed.shape[0], parts[0].shape[1]), jnp.bfloat16),
        (mask, normed, *parts),
        scalars=1,
    )


def on_device(
    residual_in,
    queries,
    keys,
    values,
    w_out,
    conv_value,
    conv_gate,
    depth_kernel,
    conv_out,
    ffn_in,
    ffn_down,
    ffn_mask,
):
    row_count = queries.shape[0]
    half = ffn_in.shape[1] // 2
    line = Line(3)
    line.add([("keys", keys, None), ("values", values, None), ("w_out", w_out, 1)])
    line.add([("value", conv_value, 0), ("gate", conv_gate, 0), ("conv_out", conv_out, 1)])
    line.add([("in_a", ffn_in[:, :half], 0), ("in_b", ffn_in[:, half:], 0)])
    line.add([("down_a", ffn_down[:half], 1), ("down_b", ffn_down[half:], 1)])
    line.begin()

    share_count = row_count // lax.axis_size("mp")
    stream = to_held_order(
        lax.dynamic_slice_in_dim(
            residual_in, lax.axis_index("mp") * share_count, share_count, 0
        )
    )
    queries = line.until(["keys", "values"], queries)
    heads_out = attention(queries, line.take("keys", 0), line.take("values", 0))
    heads_out = line.until(["w_out"], heads_out)
    sent, kept = project([heads_out], [line.take("w_out", 1)])
    stream = stream.astype(jnp.float32) + scatter_sum(sent, kept, line, (1, 2))
    norm_one = widen(layer_norm(stream).astype(jnp.bfloat16), line, (1, 2))

    norm_one = line.until(["value", "gate"], norm_one)
    units = gated(norm_one, line.take("value", 0), line.take("gate", 0))
    units = line.until(["conv_out"], units)
    sent, kept = conv_branch(units, depth_kernel, line.take("conv_out", 1))
    stream = stream + scatter_sum(sent, kept, line, (1, 1))
    norm_two = widen(layer_norm(stream).astype(jnp.bfloat16), line, (1, 1))

    blocks = ffn_mask.shape[1] // 2
    norm_two = line.until(["in_a"], norm_two)
    hidden_a = hidden_of(norm_two, line.take("in_a", 0), ffn_mask[:, :blocks])
    norm_two, hidden_a = line.until(["in_b"], (norm_two, hidden_a))
    hidden_b = hidden_of(norm_two, line.take("in_b", 0), ffn_mask[:, blocks:])
    hidden = line.until(["down_a", "down_b"], (hidden_a, hidden_b))
    sent, kept = project(hidden, [line.take("down_a", 1), line.take("down_b", 1)])
    stream = stream + 0.5 * scatter_sum(sent, kept, line, (0, 0))
    return to_natural_order(layer_norm(stream))


def solution(mesh):
    in_specs = (
        P(("dp", "seq"), None),
        P(("dp", "seq"), "mp"),
        P(("dp", "seq"), "mp"),
        P(("dp", "seq"), "mp"),
        P("mp", "seq"),
        P("seq", "mp"),
        P("seq", "mp"),
        P(None, "mp"),
        P("mp", "seq"),
        P("seq", "mp"),
        P("mp", "seq"),
        P(("dp", "seq"), "mp"),
    )
    out_specs = P(("dp", "seq", "mp"), None)
    return jax.shard_map(
        on_device, mesh=mesh, in_specs=in_specs, out_specs=out_specs, check_vma=False
    )
```

profile of v0, /device:TPU:0, one launch (start us, length us, event | category | flops | bytes accessed | tf_op | source)
XLA Modules:
  0.0 368.2 jit_solution(8638409247175590134)
XLA Ops:
  8.0 7.2 %collective-permute-done.refs_1_ = bf16[384,512]{1,0:T(8,128)(2,1)S(1)} collective-permute-done((bf16[384,512]{1,0:T(8,128)(2,1)}, bf16[384,512]{1,0:T(8,128)(2,1)S(1)}, u32[]{:S(2)}, u32[]{:S(2)}) %collective-permute-start) | collective-permute-done | bytes 393248 | tf_op jit(solution)/shard_map/ppermute | solution.py:44
  15.2 8.4 %collective-permute-done.1.refs_5_ = bf16[384,512]{1,0:T(8,128)(2,1)S(1)} collective-permute-done((bf16[384,512]{1,0:T(8,128)(2,1)}, bf16[384,512]{1,0:T(8,128)(2,1)S(1)}, u32[]{:S(2)}, u32[]{:S(2)}) %collective-permute-start.1) | collective-permute-done | bytes 393248 | tf_op jit(solution)/shard_map/ppermute | solution.py:44
  31.4 6.3 %collective-permute-done.3.refs_2_ = bf16[384,512]{1,0:T(8,128)(2,1)S(1)} collective-permute-done((bf16[384,512]{1,0:T(8,128)(2,1)S(1)}, bf16[384,512]{1,0:T(8,128)(2,1)S(1)}, u32[]{:S(2)}, u32[]{:S(2)}) %collective-permute-start.3) | collective-permute-done | bytes 393248 | tf_op jit(solution)/shard_map/ppermute | solution.py:44
  37.7 8.5 %collective-permute-done.4.refs_6_ = bf16[384,512]{1,0:T(8,128)(2,1)} collective-permute-done((bf16[384,512]{1,0:T(8,128)(2,1)S(1)}, bf16[384,512]{1,0:T(8,128)(2,1)}, u32[]{:S(2)}, u32[]{:S(2)}) %collective-permute-start.4) | collective-permute-done | bytes 393248 | tf_op jit(solution)/shard_map/ppermute | solution.py:44
  60.3 8.4 %collective-permute-done.8.refs_7_ = bf16[384,512]{1,0:T(8,128)(2,1)} collective-permute-done((bf16[384,512]{1,0:T(8,128)(2,1)}, bf16[384,512]{1,0:T(8,128)(2,1)}, u32[]{:S(2)}, u32[]{:S(2)}) %collective-permute-start.8) | collective-permute-done | bytes 393248 | tf_op jit(solution)/shard_map/ppermute | solution.py:44
  68.7 9.1 %shard_map.118.refs_0_ = bf16[384,512]{1,0:T(8,128)(2,1)} custom-call(bf16[384,512]{1,0:T(8,128)(2,1)} %q_ref, bf16[384,512]{1,0:T(8,128)(2,1)} %refs_0_.1, bf16[384,512]{1,0:T(8,128)(2,1)} %copy-done.37, bf16[384,512]{1,0:T(8,128)(2,1)} %copy-done.39, bf16[384,512]{1,0:T(8,128)(2,1)} %collective-permute-done.6.refs_3_, bf16[384,512]{1,0:T(8,128)(2,1)} %refs_4_.1, ...), custom_call_target="tpu_custom_call" | custom-call | tf_op jit(solution)/shard_map/pallas_call | solution.py:196
  100.0 6.1 %collective-permute-done.14.refs_2_ = bf16[512,256]{1,0:T(8,128)(2,1)} collective-permute-done((bf16[512,256]{1,0:T(8,128)(2,1)S(1)}, bf16[512,256]{1,0:T(8,128)(2,1)}, u32[]{:S(2)}, u32[]{:S(2)}) %collective-permute-start.14) | collective-permute-done | bytes 262176 | tf_op jit(solution)/shard_map/ppermute | solution.py:44
  131.7 9.0 %collective-permute-done.22.refs_4_ = bf16[512,256]{1,0:T(8,128)(2,1)S(1)} collective-permute-done((bf16[512,256]{1,0:T(8,128)(2,1)}, bf16[512,256]{1,0:T(8,128)(2,1)S(1)}, u32[]{:S(2)}, u32[]{:S(2)}) %collective-permute-start.22) | collective-permute-done | bytes 262176 | tf_op jit(solution)/shard_map/ppermute | solution.py:44
  149.6 7.2 %collective-permute-done.27.refs_14_ = bf16[256,512]{1,0:T(8,128)(2,1)S(1)} collective-permute-done((bf16[256,512]{1,0:T(8,128)(2,1)}, bf16[256,512]{1,0:T(8,128)(2,1)S(1)}, u32[]{:S(2)}, u32[]{:S(2)}) %collective-permute-start.27) | collective-permute-done | bytes 262176 | tf_op jit(solution)/shard_map/ppermute | solution.py:44
  163.0 10.7 %collective-permute-done.32.refs_2_ = bf16[256,1024]{1,0:T(8,128)(2,1)S(1)} collective-permute-done((bf16[256,1024]{1,0:T(8,128)(2,1)S(1)}, bf16[256,1024]{1,0:T(8,128)(2,1)S(1)}, u32[]{:S(2)}, u32[]{:S(2)}) %collective-permute-start.32) | collective-permute-done | bytes 524320 | tf_op jit(solution)/shard_map/ppermute | solution.py:44
  192.7 9.7 %shard_map.121 = (bf16[2,96,2048]{2,1,0:T(8,128)(2,1)}, f32[2,96,2048]{2,1,0:T(8,128)}) custom-call(bf16[384,512]{1,0:T(8,128)(2,1)} %shard_map.120.x_ref, bf16[16,512]{1,0:T(8,128)(2,1)} %copy-done.54, bf16[16,512]{1,0:T(8,128)(2,1)} %copy-done.55, f32[31,512]{1,0:T(8,128)} %taps_ref.1, bf16[512,256]{1,0:T(8,128)(2,1)} %copy-done.7, ...), custom_call_target="tpu_custom_call" | custom-call | tf_op jit(solution)/shard_map/pallas_call | solution.py:196
  206.7 12.3 %collective-permute-done.38.refs_4_ = bf16[256,1024]{1,0:T(8,128)(2,1)S(1)} collective-permute-done((bf16[256,1024]{1,0:T(8,128)(2,1)S(1)}, bf16[256,1024]{1,0:T(8,128)(2,1)S(1)}, u32[]{:S(2)}, u32[]{:S(2)}) %collective-permute-start.38) | collective-permute-done | bytes 524320 | tf_op jit(solution)/shard_map/ppermute | solution.py:44
  224.1 6.2 %collective-permute-done.41.refs_4_ = bf16[256,1024]{1,0:T(8,128)(2,1)S(1)} collective-permute-done((bf16[256,1024]{1,0:T(8,128)(2,1)S(1)}, bf16[256,1024]{1,0:T(8,128)(2,1)S(1)}, u32[]{:S(2)}, u32[]{:S(2)}) %collective-permute-start.41) | collective-permute-done | bytes 524320 | tf_op jit(solution)/shard_map/ppermute | solution.py:44
  234.8 6.7 %collective-permute-done.44.refs_6_ = bf16[256,1024]{1,0:T(8,128)(2,1)S(1)} collective-permute-done((bf16[256,1024]{1,0:T(8,128)(2,1)S(1)}, bf16[256,1024]{1,0:T(8,128)(2,1)S(1)}, u32[]{:S(2)}, u32[]{:S(2)}) %collective-permute-start.44) | collective-permute-done | bytes 524320 | tf_op jit(solution)/shard_map/ppermute | solution.py:44
  246.1 6.6 %collective-permute-done.47.refs_6_ = bf16[256,1024]{1,0:T(8,128)(2,1)S(1)} collective-permute-done((bf16[256,1024]{1,0:T(8,128)(2,1)S(1)}, bf16[256,1024]{1,0:T(8,128)(2,1)S(1)}, u32[]{:S(2)}, u32[]{:S(2)}) %collective-permute-start.47) | collective-permute-done | bytes 524320 | tf_op jit(solution)/shard_map/ppermute | solution.py:44
  255.2 8.8 %collective-permute-done.50.refs_4_ = bf16[1024,256]{1,0:T(8,128)(2,1)S(1)} collective-permute-done((bf16[1024,256]{1,0:T(8,128)(2,1)S(1)}, bf16[1024,256]{1,0:T(8,128)(2,1)S(1)}, u32[]{:S(2)}, u32[]{:S(2)}) %collective-permute-start.50) | collective-permute-done | bytes 524320 | tf_op jit(solution)/shard_map/ppermute | solution.py:44
  276.2 6.1 %shard_map.123.refs_1_ = bf16[384,1024]{1,0:T(8,128)(2,1)} custom-call(s32[3,8]{1,0:T(4,128)} %get-tuple-element.291.mask_ref, bf16[384,2048]{1,0:T(8,128)(2,1)} %bitcast.54, bf16[256,1024]{1,0:T(8,128)(2,1)} %copy-done.1, bf16[256,1024]{1,0:T(8,128)(2,1)} %get-tuple-element.273.refs_1_, bf16[256,1024]{1,0:T(8,128)(2,1)} %copy-done.9, ...), custom_call_target="tpu_custom_call" | custom-call | tf_op jit(solution)/shard_map/pallas_call | solution.py:196
  287.5 10.2 %collective-permute-done.56.refs_14_ = bf16[1024,256]{1,0:T(8,128)(2,1)S(1)} collective-permute-done((bf16[1024,256]{1,0:T(8,128)(2,1)S(1)}, bf16[1024,256]{1,0:T(8,128)(2,1)S(1)}, u32[]{:S(2)}, u32[]{:S(2)}) %collective-permute-start.56) | collective-permute-done | bytes 524320 | tf_op jit(solution)/shard_map/ppermute | solution.py:44
  298.7 10.2 %collective-permute-done.58.refs_8_ = bf16[1024,256]{1,0:T(8,128)(2,1)S(1)} collective-permute-done((bf16[1024,256]{1,0:T(8,128)(2,1)S(1)}, bf16[1024,256]{1,0:T(8,128)(2,1)S(1)}, u32[]{:S(2)}, u32[]{:S(2)}) %collective-permute-start.58) | collective-permute-done | bytes 524320 | tf_op jit(solution)/shard_map/ppermute | solution.py:44
  309.6 10.1 %collective-permute-done.60.refs_16_ = bf16[1024,256]{1,0:T(8,128)(2,1)S(1)} collective-permute-done((bf16[1024,256]{1,0:T(8,128)(2,1)S(1)}, bf16[1024,256]{1,0:T(8,128)(2,1)S(1)}, u32[]{:S(2)}, u32[]{:S(2)}) %collective-permute-start.60) | collective-permute-done | bytes 524320 | tf_op jit(solution)/shard_map/ppermute | solution.py:44
  320.4 9.5 %collective-permute-done.62.refs_9_ = bf16[1024,256]{1,0:T(8,128)(2,1)S(1)} collective-permute-done((bf16[1024,256]{1,0:T(8,128)(2,1)S(1)}, bf16[1024,256]{1,0:T(8,128)(2,1)S(1)}, u32[]{:S(2)}, u32[]{:S(2)}) %collective-permute-start.62) | collective-permute-done | bytes 524320 | tf_op jit(solution)/shard_map/ppermute | solution.py:70
  329.8 10.6 %collective-permute-done.63.refs_17_ = bf16[1024,256]{1,0:T(8,128)(2,1)S(1)} collective-permute-done((bf16[1024,256]{1,0:T(8,128)(2,1)S(1)}, bf16[1024,256]{1,0:T(8,128)(2,1)S(1)}, u32[]{:S(2)}, u32[]{:S(2)}) %collective-permute-start.63) | collective-permute-done | bytes 524320 | tf_op jit(solution)/shard_map/ppermute | solution.py:70
  341.2 9.3 %shard_map.124 = (bf16[2,96,2048]{2,1,0:T(8,128)(2,1)}, f32[2,96,2048]{2,1,0:T(8,128)}) custom-call(bf16[384,1024]{1,0:T(8,128)(2,1)} %shard_map.122.refs_0_, bf16[384,1024]{1,0:T(8,128)(2,1)} %shard_map.123.refs_1_, bf16[1024,256]{1,0:T(8,128)(2,1)} %copy-done.3, bf16[1024,256]{1,0:T(8,128)(2,1)} %get-tuple-element.271.refs_3_, ...), custom_call_target="tpu_custom_call" | custom-call | tf_op jit(solution)/shard_map/pallas_call | solution.py:196
  356.2 9.6 %collective-permute-done.65 = bf16[1,96,2048]{2,1,0:T(8,128)(2,1)S(1)} collective-permute-done((bf16[1,96,2048]{2,1,0:T(8,128)(2,1)S(1)}, bf16[1,96,2048]{2,1,0:T(8,128)(2,1)S(1)}, u32[]{:S(2)}, u32[]{:S(2)}) %collective-permute-start.65) | collective-permute-done | bytes 393248 | tf_op jit(solution)/shard_map/ppermute | solution.py:166
  (300 shorter events, 160.5 us)
Async XLA Ops:
  3.0 20.6 %collective-permute-start.1 = (bf16[384,512]{1,0:T(8,128)(2,1)}, bf16[384,512]{1,0:T(8,128)(2,1)S(1)}, u32[]{:S(2)}, u32[]{:S(2)}) collective-permute-start(bf16[384,512]{1,0:T(8,128)(2,1)} %refs_4_.1), channel_id=1, source_target_pairs={{0,8},{8,16},{16,24},{24,0},{1,9},{9,17},{17,25},{25,1},{2,10},{10... | collective-permute-start | bytes 1179656 | tf_op jit(solution)/shard_map/ppermute | solution.py:44
  6.4 23.0 %collective-permute-start.2 = (bf16[512,256]{1,0:T(8,128)(2,1)S(1)}, bf16[512,256]{1,0:T(8,128)(2,1)}, u32[]{:S(2)}, u32[]{:S(2)}) collective-permute-start(bf16[512,256]{1,0:T(8,128)(2,1)S(1)} %get-tuple-element.288.refs_1_), channel_id=1, source_target_pairs={{0,8},{8,16},{16,24},{24,0},{1,9},{9,17},{17,25},{25,1},{2,10},{10... | collective-permute-start | bytes 786440 | tf_op jit(solution)/shard_map/ppermute | solution.py:44
  23.7 22.5 %collective-permute-start.4 = (bf16[384,512]{1,0:T(8,128)(2,1)S(1)}, bf16[384,512]{1,0:T(8,128)(2,1)}, u32[]{:S(2)}, u32[]{:S(2)}) collective-permute-start(bf16[384,512]{1,0:T(8,128)(2,1)S(1)} %collective-permute-done.1.refs_5_), channel_id=1, source_target_pairs={{0,8},{8,16},{16,24},{24,0},{1,9},{9,17},{17,25},{25,1},{2,10},{10... | collective-permute-start | bytes 1179656 | tf_op jit(solution)/shard_map/ppermute | solution.py:44
  29.4 22.5 %collective-permute-start.5 = (bf16[512,256]{1,0:T(8,128)(2,1)}, bf16[512,256]{1,0:T(8,128)(2,1)}, u32[]{:S(2)}, u32[]{:S(2)}) collective-permute-start(bf16[512,256]{1,0:T(8,128)(2,1)} %collective-permute-done.2.refs_3_), channel_id=1, source_target_pairs={{0,8},{8,16},{16,24},{24,0},{1,9},{9,17},{17,25},{25,1},{2,10},{10... | collective-permute-start | bytes 786440 | tf_op jit(solution)/shard_map/ppermute | solution.py:44
  46.2 22.4 %collective-permute-start.8 = (bf16[384,512]{1,0:T(8,128)(2,1)}, bf16[384,512]{1,0:T(8,128)(2,1)}, u32[]{:S(2)}, u32[]{:S(2)}) collective-permute-start(bf16[384,512]{1,0:T(8,128)(2,1)} %collective-permute-done.4.refs_6_), channel_id=1, source_target_pairs={{0,8},{8,16},{16,24},{24,0},{1,9},{9,17},{17,25},{25,1},{2,10},{10... | collective-permute-start | bytes 1179656 | tf_op jit(solution)/shard_map/ppermute | solution.py:44
  51.8 26.0 %collective-permute-start.9 = (bf16[512,256]{1,0:T(8,128)(2,1)}, bf16[512,256]{1,0:T(8,128)(2,1)}, u32[]{:S(2)}, u32[]{:S(2)}) collective-permute-start(bf16[512,256]{1,0:T(8,128)(2,1)} %collective-permute-done.5.refs_5_), channel_id=1, source_target_pairs={{0,8},{8,16},{16,24},{24,0},{1,9},{9,17},{17,25},{25,1},{2,10},{10... | collective-permute-start | bytes 786440 | tf_op jit(solution)/shard_map/ppermute | solution.py:44
  54.5 28.1 %collective-permute-start.11 = (bf16[512,256]{1,0:T(8,128)(2,1)}, bf16[512,256]{1,0:T(8,128)(2,1)S(1)}, u32[]{:S(2)}, u32[]{:S(2)}) collective-permute-start(bf16[512,256]{1,0:T(8,128)(2,1)} %collective-permute-done.5.refs_5_), channel_id=1, source_target_pairs={{0,1},{1,0},{2,3},{3,2},{4,5},{5,4},{6,7},{7,6},{8,9},{9,8},{10,11... | collective-permute-start | bytes 786440 | tf_op jit(solution)/shard_map/ppermute | solution.py:70
  60.3 22.4 %collective-permute-start.10 = (bf16[256,512]{1,0:T(8,128)(2,1)S(1)}, bf16[256,512]{1,0:T(8,128)(2,1)}, u32[]{:S(2)}, u32[]{:S(2)}) collective-permute-start(bf16[256,512]{1,0:T(8,128)(2,1)S(1)} %get-tuple-element.154.refs_0_), channel_id=1, source_target_pairs={{0,8},{8,16},{16,24},{24,0},{1,9},{9,17},{17,25},{25,1},{2,10},{10... | collective-permute-start | bytes 786440 | tf_op jit(solution)/shard_map/ppermute | solution.py:44
  157.4 27.0 %collective-permute-start.34 = (bf16[256,1024]{1,0:T(8,128)(2,1)S(1)}, bf16[256,1024]{1,0:T(8,128)(2,1)S(1)}, u32[]{:S(2)}, u32[]{:S(2)}) collective-permute-start(bf16[256,1024]{1,0:T(8,128)(2,1)S(1)} %get-tuple-element.194.refs_0_), channel_id=1, source_target_pairs={{0,8},{8,16},{16,24},{24,0},{1,9},{9,17},{17,25},{25,1},{2,10},{10... | collective-permute-start | bytes 1572872 | tf_op jit(solution)/shard_map/ppermute | solution.py:44
  162.4 22.1 %collective-permute-start.35 = (bf16[512,256]{1,0:T(8,128)(2,1)S(1)}, bf16[512,256]{1,0:T(8,128)(2,1)S(1)}, u32[]{:S(2)}, u32[]{:S(2)}) collective-permute-start(bf16[512,256]{1,0:T(8,128)(2,1)S(1)} %collective-permute-done.30.refs_6_), channel_id=1, source_target_pairs={{0,1},{1,0},{2,3},{3,2},{4,5},{5,4},{6,7},{7,6},{8,9},{9,8},{10,11... | collective-permute-start | bytes 786440 | tf_op jit(solution)/shard_map/ppermute | solution.py:70
  203.3 27.0 %collective-permute-start.42 = (bf16[256,1024]{1,0:T(8,128)(2,1)S(1)}, bf16[256,1024]{1,0:T(8,128)(2,1)S(1)}, u32[]{:S(2)}, u32[]{:S(2)}) collective-permute-start(bf16[256,1024]{1,0:T(8,128)(2,1)S(1)} %collective-permute-done.34.refs_2_), channel_id=1, source_target_pairs={{0,1},{1,0},{2,3},{3,2},{4,5},{5,4},{6,7},{7,6},{8,9},{9,8},{10,11... | collective-permute-start | bytes 1572872 | tf_op jit(solution)/shard_map/ppermute | solution.py:70
  204.7 25.5 %collective-permute-start.41 = (bf16[256,1024]{1,0:T(8,128)(2,1)S(1)}, bf16[256,1024]{1,0:T(8,128)(2,1)S(1)}, u32[]{:S(2)}, u32[]{:S(2)}) collective-permute-start(bf16[256,1024]{1,0:T(8,128)(2,1)S(1)} %collective-permute-done.34.refs_2_), channel_id=1, source_target_pairs={{0,8},{8,16},{16,24},{24,0},{1,9},{9,17},{17,25},{25,1},{2,10},{10... | collective-permute-start | bytes 1572872 | tf_op jit(solution)/shard_map/ppermute | solution.py:44
  252.7 22.5 %collective-permute-start.52 = (bf16[1024,256]{1,0:T(8,128)(2,1)S(1)}, bf16[1024,256]{1,0:T(8,128)(2,1)S(1)}, u32[]{:S(2)}, u32[]{:S(2)}) collective-permute-start(bf16[1024,256]{1,0:T(8,128)(2,1)S(1)} %get-tuple-element.220.refs_10_), channel_id=1, source_target_pairs={{0,8},{8,16},{16,24},{24,0},{1,9},{9,17},{17,25},{25,1},{2,10},{10... | collective-permute-start | bytes 1572872 | tf_op jit(solution)/shard_map/ppermute | solution.py:44
  252.8 22.5 %collective-permute-start.53 = (bf16[256,1024]{1,0:T(8,128)(2,1)S(1)}, bf16[256,1024]{1,0:T(8,128)(2,1)S(1)}, u32[]{:S(2)}, u32[]{:S(2)}) collective-permute-start(bf16[256,1024]{1,0:T(8,128)(2,1)S(1)} %collective-permute-done.47.refs_6_), channel_id=1, source_target_pairs={{0,1},{1,0},{2,3},{3,2},{4,5},{5,4},{6,7},{7,6},{8,9},{9,8},{10,11... | collective-permute-start | bytes 1572872 | tf_op jit(solution)/shard_map/ppermute | solution.py:70
  264.0 22.5 %collective-permute-start.55 = (bf16[1024,256]{1,0:T(8,128)(2,1)S(1)}, bf16[1024,256]{1,0:T(8,128)(2,1)S(1)}, u32[]{:S(2)}, u32[]{:S(2)}) collective-permute-start(bf16[1024,256]{1,0:T(8,128)(2,1)S(1)} %collective-permute-done.50.refs_4_), channel_id=1, source_target_pairs={{0,1},{1,0},{2,3},{3,2},{4,5},{5,4},{6,7},{7,6},{8,9},{9,8},{10,11... | collective-permute-start | bytes 1572872 | tf_op jit(solution)/shard_map/ppermute | solution.py:70
  264.6 21.8 %collective-permute-start.54 = (bf16[1024,256]{1,0:T(8,128)(2,1)S(1)}, bf16[1024,256]{1,0:T(8,128)(2,1)S(1)}, u32[]{:S(2)}, u32[]{:S(2)}) collective-permute-start(bf16[1024,256]{1,0:T(8,128)(2,1)S(1)} %collective-permute-done.50.refs_4_), channel_id=1, source_target_pairs={{0,8},{8,16},{16,24},{24,0},{1,9},{9,17},{17,25},{25,1},{2,10},{10... | collective-permute-start | bytes 1572872 | tf_op jit(solution)/shard_map/ppermute | solution.py:44
  275.2 22.5 %collective-permute-start.56 = (bf16[1024,256]{1,0:T(8,128)(2,1)S(1)}, bf16[1024,256]{1,0:T(8,128)(2,1)S(1)}, u32[]{:S(2)}, u32[]{:S(2)}) collective-permute-start(bf16[1024,256]{1,0:T(8,128)(2,1)S(1)} %collective-permute-done.52.refs_12_), channel_id=1, source_target_pairs={{0,8},{8,16},{16,24},{24,0},{1,9},{9,17},{17,25},{25,1},{2,10},{10... | collective-permute-start | bytes 1572872 | tf_op jit(solution)/shard_map/ppermute | solution.py:44
  275.7 22.0 %collective-permute-start.57 = (bf16[1024,256]{1,0:T(8,128)(2,1)S(1)}, bf16[1024,256]{1,0:T(8,128)(2,1)S(1)}, u32[]{:S(2)}, u32[]{:S(2)}) collective-permute-start(bf16[1024,256]{1,0:T(8,128)(2,1)S(1)} %collective-permute-done.52.refs_12_), channel_id=1, source_target_pairs={{0,1},{1,0},{2,3},{3,2},{4,5},{5,4},{6,7},{7,6},{8,9},{9,8},{10,11... | collective-permute-start | bytes 1572872 | tf_op jit(solution)/shard_map/ppermute | solution.py:70
  286.5 22.5 %collective-permute-start.59 = (bf16[1024,256]{1,0:T(8,128)(2,1)S(1)}, bf16[1024,256]{1,0:T(8,128)(2,1)S(1)}, u32[]{:S(2)}, u32[]{:S(2)}) collective-permute-start(bf16[1024,256]{1,0:T(8,128)(2,1)S(1)} %collective-permute-done.54.refs_6_), channel_id=1, source_target_pairs={{0,1},{1,0},{2,3},{3,2},{4,5},{5,4},{6,7},{7,6},{8,9},{9,8},{10,11... | collective-permute-start | bytes 1572872 | tf_op jit(solution)/shard_map/ppermute | solution.py:70
  287.1 21.8 %collective-permute-start.58 = (bf16[1024,256]{1,0:T(8,128)(2,1)S(1)}, bf16[1024,256]{1,0:T(8,128)(2,1)S(1)}, u32[]{:S(2)}, u32[]{:S(2)}) collective-permute-start(bf16[1024,256]{1,0:T(8,128)(2,1)S(1)} %collective-permute-done.54.refs_6_), channel_id=1, source_target_pairs={{0,8},{8,16},{16,24},{24,0},{1,9},{9,17},{17,25},{25,1},{2,10},{10... | collective-permute-start | bytes 1572872 | tf_op jit(solution)/shard_map/ppermute | solution.py:44
  297.7 22.0 %collective-permute-start.60 = (bf16[1024,256]{1,0:T(8,128)(2,1)S(1)}, bf16[1024,256]{1,0:T(8,128)(2,1)S(1)}, u32[]{:S(2)}, u32[]{:S(2)}) collective-permute-start(bf16[1024,256]{1,0:T(8,128)(2,1)S(1)} %collective-permute-done.56.refs_14_), channel_id=1, source_target_pairs={{0,8},{8,16},{16,24},{24,0},{1,9},{9,17},{17,25},{25,1},{2,10},{10... | collective-permute-start | bytes 1572872 | tf_op jit(solution)/shard_map/ppermute | solution.py:44
  298.1 21.6 %collective-permute-start.61 = (bf16[1024,256]{1,0:T(8,128)(2,1)S(1)}, bf16[1024,256]{1,0:T(8,128)(2,1)S(1)}, u32[]{:S(2)}, u32[]{:S(2)}) collective-permute-start(bf16[1024,256]{1,0:T(8,128)(2,1)S(1)} %collective-permute-done.56.refs_14_), channel_id=1, source_target_pairs={{0,1},{1,0},{2,3},{3,2},{4,5},{5,4},{6,7},{7,6},{8,9},{9,8},{10,11... | collective-permute-start | bytes 1572872 | tf_op jit(solution)/shard_map/ppermute | solution.py:70
  308.9 20.9 %collective-permute-start.62 = (bf16[1024,256]{1,0:T(8,128)(2,1)S(1)}, bf16[1024,256]{1,0:T(8,128)(2,1)S(1)}, u32[]{:S(2)}, u32[]{:S(2)}) collective-permute-start(bf16[1024,256]{1,0:T(8,128)(2,1)S(1)} %collective-permute-done.58.refs_8_), channel_id=1, source_target_pairs={{0,1},{1,0},{2,3},{3,2},{4,5},{5,4},{6,7},{7,6},{8,9},{9,8},{10,11... | collective-permute-start | bytes 1572872 | tf_op jit(solution)/shard_map/ppermute | solution.py:70
  319.7 20.7 %collective-permute-start.63 = (bf16[1024,256]{1,0:T(8,128)(2,1)S(1)}, bf16[1024,256]{1,0:T(8,128)(2,1)S(1)}, u32[]{:S(2)}, u32[]{:S(2)}) collective-permute-start(bf16[1024,256]{1,0:T(8,128)(2,1)S(1)} %collective-permute-done.60.refs_16_), channel_id=1, source_target_pairs={{0,1},{1,0},{2,3},{3,2},{4,5},{5,4},{6,7},{7,6},{8,9},{9,8},{10,11... | collective-permute-start | bytes 1572872 | tf_op jit(solution)/shard_map/ppermute | solution.py:70
  (100 other events, 1458.5 us)
where the time goes:
time: 369 us; the launch traced here: 368 us
  waiting for transfers between devices  225 us (61%)
  Pallas kernels  50.2 us (14%)
  starting transfers between devices  47 us (13%)
  local copies, waits for them, and re-layouts  37.5 us (10%)
  other arithmetic  7.68 us (2%)
    ppermute x30, waiting for transfers between devices, start(): lax.ppermute(piece, 'seq', ring_pairs('seq'))  179 us
    pallas_call x7, Pallas kernels, kernel_call(): pl.pallas_call(kernel, out_shape=outs, in_specs=[pl.BlockSpec(memory_spac...  50.2 us
    ppermute x24, waiting for transfers between devices, visit(): piece = lax.ppermute(piece, 'dp', ring_pairs('dp'))  27.8 us
    ppermute x24, starting transfers between devices, visit(): piece = lax.ppermute(piece, 'dp', ring_pairs('dp'))  21.7 us
    unnamed x137, local copies, waits for them, and re-layouts  20.2 us
    ppermute x30, starting transfers between devices, start(): lax.ppermute(piece, 'seq', ring_pairs('seq'))  15.7 us
    ppermute x6, waiting for transfers between devices, scatter_sum(): taken = lax.ppermute(sent, 'mp', xor_pairs(count, bit))  13.7 us
    dynamic_slice x8, local copies, waits for them, and re-layouts, part_of(): return lax.dynamic_slice_in_dim(weight, index * width, width, axis=dim)  7.69 us
  transfers between devices with their start and end apart: 66, of which 38 were waited for; matrix products, arithmetic and copies ran while one was open for 9% of the time, Pallas kernels for 7%

commit v1 on v0

v1 whole, which is shorter than its diff:
```python
import functools
import math

import jax
import jax.numpy as jnp
from jax import lax
from jax.experimental import pallas as pl
from jax.experimental.pallas import tpu as pltpu
from jax.sharding import PartitionSpec as P

HEAD_DIM = 128


norm_epsilon = 1e-05


def ring_pairs(axis):
    count = lax.axis_size(axis)
    return [(i, (i + 1) % count) for i in range(count)]


class Rows:
    def __init__(self, array, first, count, block=None):
        self.array, self.first, self.count, self.block = array, first, count, block
        self.shape = (count, array.shape[1])

    def __getitem__(self, columns):
        if self.block is None:
            return self.array[self.first : self.first + self.count, columns]
        t, rows = self.block
        size = lax.axis_size("seq")
        start = lax.rem(lax.axis_index("seq") + (size - t), size) * rows + self.first
        return self.array[pl.ds(pl.multiple_of(start, math.gcd(rows, self.first)), self.count), columns]


class Line:
    def __init__(self, depth, lag):
        self.depth, self.lag = depth, lag
        self.waiting, self.under_way, self.crossing = [], [], []
        self.parts, self.pieces, self.token = {}, {}, None

    def add(self, first, last, *stream):
        by_width = {}
        for name, array in stream:
            self.parts[name, 0] = [Rows(array, 0, array.shape[0])]
            by_width.setdefault(array.shape[1], []).append((name, array))
        count, here = lax.axis_size("dp"), lax.axis_index("dp")
        steps = lax.axis_size("seq") - 1
        for held in by_width.values():
            fields = tuple((name, array.shape[0] // count) for name, array in held)
            own = [
                lax.dynamic_slice_in_dim(array, here * rows, rows, axis=0)
                for (_, array), (_, rows) in zip(held, fields)
            ]
            self.pieces[fields, 0] = own[0] if len(own) == 1 else jnp.concatenate(own, axis=0)
            for t in range(1, steps + 1):
                place = first + (last - first) * (t - 1) / max(steps - 1, 1)
                self.waiting.append((place, fields, t))

    def begin(self):
        self.waiting.sort(key=lambda step: step[0])
        self.refill()

    def refill(self):
        while self.waiting and len(self.under_way) < self.depth:
            _, fields, t = self.waiting[0]
            if (fields, t - 1) not in self.pieces:
                return
            del self.waiting[0]
            piece = self.pieces[fields, t - 1]
            if self.token is not None:
                piece, _ = lax.optimization_barrier((piece, self.token))
            self.under_way.append((fields, t, lax.ppermute(piece, "seq", ring_pairs("seq"))))

    def note(self, fields, t, piece):
        first = 0
        for name, rows in fields:
            self.parts.setdefault((name, t), []).append(Rows(piece, first, rows))
            first += rows

    def visit(self, beside):
        lag = self.lag if self.under_way else 0
        taken = self.crossing.pop(0) if len(self.crossing) > lag else None
        crossed = taken[2] if taken else None
        if self.under_way:
            fields, t, piece = self.under_way.pop(0)
            beside, piece, crossed = lax.optimization_barrier((beside, piece, crossed))
            self.token = self.pieces[fields, t] = piece
            self.note(fields, t, piece)
            self.refill()
            for _ in range(1, lax.axis_size("dp")):
                piece = lax.ppermute(piece, "dp", ring_pairs("dp"))
                self.crossing.append((fields, t, piece))
        else:
            beside, crossed = lax.optimization_barrier((beside, crossed))
        if taken:
            self.note(taken[0], taken[1], crossed)
        return beside

    def cross(self, beside):
        fields, t, taken = self.crossing.pop(0)
        beside, taken = lax.optimization_barrier((beside, taken))
        self.note(fields, t, taken)
        return beside

    def visits(self, number, beside):
        for _ in range(number * (lax.axis_size("seq") - 1) // 3):
            beside = self.visit(beside)
        return beside

    def until(self, names, beside, first=0, last=None):
        last = lax.axis_size("seq") if last is None else last
        wanted = [(name, t) for name in names for t in range(max(first, 1), last)]
        while any(len(self.parts.get(key, ())) < lax.axis_size("dp") for key in wanted):
            arrived = all(key in self.parts for key in wanted)
            beside = self.cross(beside) if arrived else self.visit(beside)
        return beside

    def take(self, name, first=0, last=None):
        last = lax.axis_size("seq") if last is None else last
        here, count = lax.axis_index("dp"), lax.axis_size("dp")
        blocks = []
        for t in range(first, last):
            parts = self.parts[name, t]
            if len(parts) > 1 and parts[0].shape[0] % 128:
                held = jnp.stack([part[:] for part in parts])
                whole = jnp.concatenate(
                    [
                        lax.dynamic_index_in_dim(held, (here - q) % count, 0, keepdims=False)
                        for q in range(count)
                    ],
                    axis=0,
                )
                parts = [Rows(whole, 0, whole.shape[0])]
            blocks.append(parts)
        return blocks


class Gathered:
    def __init__(self, token, array):
        self.rows = array.shape[0]
        if token is not None:
            array, _ = lax.optimization_barrier((array, token))
        self.array = lax.all_gather(array, "seq", axis=0, tiled=True)

    def end(self, beside):
        beside, self.array = lax.optimization_barrier((beside, self.array))
        return beside

    def take(self):
        return [
            [Rows(self.array, 0, self.rows, (t, self.rows))] for t in range(lax.axis_size("seq"))
        ]


def packed(weights):
    arrays, places = [], {}

    def place(item):
        if isinstance(item, list):
            return [place(inner) for inner in item]
        if id(item.array) not in places:
            places[id(item.array)] = len(arrays)
            arrays.append(item.array)
        return places[id(item.array)], item.first, item.count, item.block

    spec = place(weights)
    return arrays, spec


def unpacked(spec, refs):
    if isinstance(spec, list):
        return [unpacked(inner, refs) for inner in spec]
    return Rows(refs[spec[0]], *spec[1:])


def layer_norm(stream):
    row_mean = jnp.mean(stream, axis=-1, keepdims=True)
    centered = stream - row_mean
    spread_of = jnp.mean(centered * centered, axis=-1, keepdims=True)
    return centered * lax.rsqrt(spread_of + norm_epsilon)


def dot(left, right):
    return jnp.dot(left, right, preferred_element_type=jnp.float32)


def xor_pairs(count, bit):
    return [(i, i ^ bit) for i in range(count)]


def fenced(function, *values):
    outs = jax.eval_shape(function, *values)
    return lax.cond(
        lax.axis_index("seq") < lax.axis_size("seq"),
        function,
        lambda *_: jax.tree.map(lambda out: jnp.zeros(out.shape, out.dtype), outs),
        *values,
    )


def scatter_sum(sent, kept):
    count = lax.axis_size("mp")
    me = lax.axis_index("mp")
    bit = 1
    while True:
        taken = lax.ppermute(sent, "mp", xor_pairs(count, bit))
        bit *= 2
        if bit == count:
            return kept[0], taken[0]
        part = kept + taken.astype(jnp.float32)
        groups = part.reshape(-1, 2, *part.shape[1:])
        mine = (me // bit) % 2
        sent = lax.dynamic_index_in_dim(groups, 1 - mine, 1, keepdims=False).astype(jnp.bfloat16)
        kept = lax.dynamic_index_in_dim(groups, mine, 1, keepdims=False)


def widen(rows):
    count = lax.axis_size("mp")
    me = lax.axis_index("mp")
    share, width = rows.shape
    bit = count // 2
    held = rows[None]
    while bit:
        taken = lax.ppermute(held, "mp", xor_pairs(count, bit))
        first = (me // bit) % 2 == 0
        held = jnp.stack(
            [jnp.where(first, held, taken), jnp.where(first, taken, held)], axis=1
        ).reshape(-1, share, width)
        bit //= 2
    return held.reshape(count * share, width)


def swap(value, axis, bit):
    return lax.ppermute(value, axis, xor_pairs(lax.axis_size(axis), bit))


def rows_of_all(rows):
    half = rows.shape[0] // 2
    across, along = swap(rows, "dp", 1), swap(rows, "mp", 2)
    first, second = swap(across[:half], "mp", 2), swap(along[half:], "dp", 1)
    mine = jnp.concatenate([rows, along, across, first, second], axis=0)
    return mine, swap(mine, "mp", 1)


def place_rows(x_ref, mine_ref, theirs_ref):
    share = mine_ref.shape[0] // 4
    here, me = lax.axis_index("dp"), lax.axis_index("mp")
    for core, ref in enumerate((mine_ref, theirs_ref)):
        for part in range(2):
            for chip in range(2):
                m = lax.rem(me // 2 + chip, 2) * 2 + lax.rem(me + core, 2)
                first = (lax.rem(here + part, 2) * 4 + m) * share
                held = (2 * part + chip) * share
                x_ref[pl.ds(pl.multiple_of(first, share), share), :] = ref[held : held + share, :]


def sum_over_all(sent, kept):
    taken = swap(sent, "mp", 1)
    total = kept + taken.astype(jnp.float32)
    here, chip = lax.axis_index("dp"), lax.axis_index("mp") // 2

    def share(part, other):
        held = lax.dynamic_index_in_dim(total, part, 0, keepdims=False)
        return lax.dynamic_index_in_dim(held, other, 0, keepdims=False)

    far = share(1 - here, 1 - chip).astype(jnp.bfloat16)
    half = far.shape[0] // 2
    for_along, for_across = swap(far[:half], "dp", 1), swap(far[half:], "mp", 2)
    along, across = share(here, 1 - chip), share(1 - here, chip)
    along = jnp.concatenate([along[:half] + for_along.astype(jnp.float32), along[half:]], axis=0)
    across = jnp.concatenate(
        [across[:half], across[half:] + for_across.astype(jnp.float32)], axis=0
    )
    return (
        share(here, chip),
        swap(across.astype(jnp.bfloat16), "dp", 1),
        swap(along.astype(jnp.bfloat16), "mp", 2),
    )


def kernel_call(kernel, outs, args, scratch=(), scalars=0):
    return pl.pallas_call(
        kernel,
        out_shape=outs,
        in_specs=[pl.BlockSpec(memory_space=pltpu.SMEM)] * scalars
        + [pl.BlockSpec(memory_space=pltpu.VMEM)] * (len(args) - scalars),
        out_specs=jax.tree.map(lambda _: pl.BlockSpec(memory_space=pltpu.VMEM), outs),
        scratch_shapes=scratch,
        compiler_params=pltpu.CompilerParams(vmem_limit_bytes=56 * 1024 * 1024),
    )(*args)


def attend(q, key_blocks, value_blocks):
    scores = [
        lax.dot_general(
            q, keys, (((1,), (1,)), ((), ())), preferred_element_type=jnp.float32
        )
        for keys in key_blocks
    ]
    top = functools.reduce(jnp.maximum, [jnp.max(s, axis=1, keepdims=True) for s in scores])
    factor = math.log2(math.e) / math.sqrt(HEAD_DIM)
    weights = [jnp.exp2((s - top) * factor) for s in scores]
    total = sum(jnp.sum(w, axis=1, keepdims=True) for w in weights)
    mixed = sum(dot(w.astype(jnp.bfloat16), v) for w, v in zip(weights, value_blocks))
    return mixed / total


def attention_kernel(count, q_ref, *refs):
    k_refs, v_refs, o_ref = refs[:count], refs[count : 2 * count], refs[2 * count]
    rows, width = q_ref.shape
    block = 128 if rows % 128 == 0 else rows

    @pl.loop(0, rows // block)
    def _(r):
        here = pl.ds(pl.multiple_of(r * block, block), block)
        for first in range(0, width, HEAD_DIM):
            columns = slice(first, first + HEAD_DIM)
            o_ref[here, columns] = attend(
                q_ref[here, columns],
                [k_ref[:, columns] for k_ref in k_refs],
                [v_ref[:, columns] for v_ref in v_refs],
            ).astype(o_ref.dtype)


def gathered_pieces(array):
    pieces = [array]
    for _ in range(lax.axis_size("seq") - 1):
        pieces.append(lax.ppermute(pieces[-1], "seq", ring_pairs("seq")))
    return pieces


def attention(queries, keys, values):
    key_pieces, value_pieces = gathered_pieces(keys), gathered_pieces(values)
    return kernel_call(
        functools.partial(attention_kernel, len(key_pieces)),
        jax.ShapeDtypeStruct(queries.shape, jnp.bfloat16),
        (queries, *key_pieces, *value_pieces),
    )


def block_columns(t, width):
    count = lax.axis_size("seq")
    block = lax.rem(lax.axis_index("seq") + (count - t), count)
    return pl.ds(pl.multiple_of(block * width, width), width)


def stream_kernel(natural, factor, stream_ref, kept_ref, taken_ref, next_ref, norm_ref):
    width = stream_ref.shape[1] // lax.axis_size("seq")
    for t in range(lax.axis_size("seq")):
        held = slice(t * width, (t + 1) * width)
        old = stream_ref[:, block_columns(t, width) if natural else held].astype(jnp.float32)
        next_ref[:, held] = old + factor * (
            kept_ref[:, held] + taken_ref[:, held].astype(jnp.float32)
        )
    norm_ref[...] = layer_norm(next_ref[...]).astype(norm_ref.dtype)


def advance(stream, kept, taken, natural):
    return kernel_call(
        functools.partial(stream_kernel, natural, 1.0),
        (
            jax.ShapeDtypeStruct(kept.shape, jnp.float32),
            jax.ShapeDtypeStruct(kept.shape, jnp.bfloat16),
        ),
        (stream, kept, taken),
    )


def last_kernel(pieces, stream_ref, *refs):
    out_ref, next_ref = refs[-2:]
    count = lax.axis_size("seq")
    width = stream_ref.shape[1] // count
    each = len(refs[:-2]) // pieces
    for t in range(count):
        first = t * width
        for c in range(pieces):
            terms = refs[c * each : (c + 1) * each]
            wide = terms[0].shape[1] // count
            held = slice(t * wide, (t + 1) * wide)
            total = sum(term[:, held].astype(jnp.float32) for term in terms)
            place = slice(first, first + wide)
            next_ref[:, place] = stream_ref[:, place] + 0.5 * total
            first += wide
    next_ref[...] = layer_norm(next_ref[...])
    for t in range(count):
        out_ref[:, block_columns(t, width)] = next_ref[:, t * width : (t + 1) * width]


def finish(stream, pieces):
    return kernel_call(
        functools.partial(last_kernel, len(pieces)),
        jax.ShapeDtypeStruct(stream.shape, jnp.float32),
        (stream, *[term for terms in pieces for term in terms]),
        [pltpu.VMEM(stream.shape, jnp.float32)],
    )


def part_columns(base, parts):
    rows, count = parts[0].shape[0], len(parts)
    if count == 1:
        return [slice(base, base + rows)]
    here = lax.axis_index("dp")
    return [
        pl.ds(pl.multiple_of(base + lax.rem(here + (count - p), count) * rows, rows), rows)
        for p in range(count)
    ]


def share_out(product_ref, sent_ref, kept_ref, columns):
    lead, share = sent_ref.shape[:-2], sent_ref.shape[-2]
    mine = lax.axis_index("mp") % 2
    for j in range(math.prod(lead)):
        theirs = pl.ds(pl.multiple_of((2 * j + 1 - mine) * share, share), share)
        ours = pl.ds(pl.multiple_of((2 * j + mine) * share, share), share)
        place = (j,) if len(lead) == 1 else (j // lead[1], j % lead[1])
        sent_ref[(*place, slice(None), columns)] = product_ref[theirs, :].astype(sent_ref.dtype)
        kept_ref[(*place, slice(None), columns)] = product_ref[ours, :]


def met(x_ref, base, parts, columns):
    return [
        dot(x_ref[:, held], part[columns]) for held, part in zip(part_columns(base, parts), parts)
    ]


def project_refs(left, weights, sent_ref, kept_ref, product_ref):
    width = product_ref.shape[1]
    for t in range(len(weights[0])):
        terms, base = [], 0
        for weight in weights:
            terms.extend(met(left, base, weight[t], slice(None)))
            base += sum(part.shape[0] for part in weight[t])
        product_ref[...] = sum(terms)
        share_out(product_ref, sent_ref, kept_ref, slice(t * width, (t + 1) * width))


def project_kernel(spec, left_ref, *refs):
    project_refs(left_ref, unpacked(spec, refs[:-3]), *refs[-3:])


def shares(rows, columns):
    count = lax.axis_size("mp")
    shape = (count // 2, rows // count, columns)
    return (
        jax.ShapeDtypeStruct(shape, jnp.bfloat16),
        jax.ShapeDtypeStruct(shape, jnp.float32),
    )


def project(left, weights):
    rows, width, number = left.shape[0], weights[0][0][0].shape[1], len(weights[0])
    arrays, spec = packed(weights)
    return kernel_call(
        functools.partial(project_kernel, spec),
        shares(rows, width * number),
        (left, *arrays),
        [pltpu.VMEM((rows, width), jnp.float32)],
    )


def heads_kernel(spec, piece_count, *refs):
    pieces, (sent_ref, kept_ref, left_ref, product_ref) = refs[:piece_count], refs[-4:]
    width = pieces[0].shape[1]
    for d, piece in enumerate(pieces):
        head = lax.rem(lax.axis_index("seq") + d, piece_count)
        left_ref[:, pl.ds(pl.multiple_of(head * width, width), width)] = piece[...]
    project_refs(left_ref, unpacked(spec, refs[piece_count:-4]), sent_ref, kept_ref, product_ref)


def project_heads(pieces, weights):
    rows, width, number = pieces[0].shape[0], weights[0][0][0].shape[1], len(weights[0])
    arrays, spec = packed(weights)
    return kernel_call(
        functools.partial(heads_kernel, spec, len(pieces)),
        shares(rows, width * number),
        (*pieces, *arrays),
        [
            pltpu.VMEM((rows, pieces[0].shape[1] * len(pieces)), jnp.bfloat16),
            pltpu.VMEM((rows, width), jnp.float32),
        ],
    )


def pack_kernel(q_ref, k_ref, v_ref, *out_refs):
    count = len(out_refs)
    width = q_ref.shape[1] // count
    for d, out_ref in enumerate(out_refs):
        head = lax.rem(lax.axis_index("seq") + d, count)
        columns = pl.ds(pl.multiple_of(head * width, width), width)
        for i, ref in enumerate((q_ref, k_ref, v_ref)):
            out_ref[:, i * width : (i + 1) * width] = ref[:, columns]


def heads_by_device(queries, keys, values):
    count = lax.axis_size("seq")
    rows, columns = queries.shape
    pieces = kernel_call(
        pack_kernel,
        [jax.ShapeDtypeStruct((rows, 3 * columns // count), queries.dtype)] * count,
        (queries, keys, values),
    )
    return [pieces[0]] + [
        lax.ppermute(pieces[d], "seq", [(i, (i + d) % count) for i in range(count)])
        for d in range(1, count)
    ]


def heads_kernel_of_all(*refs):
    count = len(refs) // 2
    width = refs[0].shape[1] // 3
    rows = refs[0].shape[0]
    block = 128 if rows % 128 == 0 else rows
    for first in range(0, width, HEAD_DIM):
        columns = [slice(i * width + first, i * width + first + HEAD_DIM) for i in range(3)]
        for in_ref, o_ref in zip(refs[:count], refs[count:]):

            @pl.loop(0, rows // block)
            def _(r):
                here = pl.ds(pl.multiple_of(r * block, block), block)
                o_ref[here, first : first + HEAD_DIM] = attend(
                    in_ref[here, columns[0]],
                    [ref[:, columns[1]] for ref in refs[:count]],
                    [ref[:, columns[2]] for ref in refs[:count]],
                ).astype(o_ref.dtype)


def attention_by_head(pieces):
    rows, columns = pieces[0].shape
    return kernel_call(
        heads_kernel_of_all,
        [jax.ShapeDtypeStruct((rows, columns // 3), jnp.bfloat16)] * len(pieces),
        tuple(pieces),
    )


def through(x_ref, weight, columns):
    width = sum(part.shape[0] for part in weight[0])
    return sum(
        term for t, parts in enumerate(weight) for term in met(x_ref, t * width, parts, columns)
    )


def column_tiles(width):
    tile = 256 if width % 256 == 0 else width
    return width // tile, tile


def gated_kernel(spec, x_ref, *refs):
    value, gate_weight = unpacked(spec, refs[:-1])
    o_ref = refs[-1]
    tiles, tile = column_tiles(o_ref.shape[1])

    @pl.loop(0, tiles)
    def _(n):
        columns = pl.ds(pl.multiple_of(n * tile, tile), tile)
        gate = through(x_ref, gate_weight, columns)
        o_ref[:, columns] = (
            through(x_ref, value, columns) / (1.0 + jnp.exp(-gate))
        ).astype(o_ref.dtype)


def gated(normed, value, gate):
    arrays, spec = packed([value, gate])
    return kernel_call(
        functools.partial(gated_kernel, spec),
        jax.ShapeDtypeStruct((normed.shape[0], value[0][0].shape[1]), jnp.bfloat16),
        (normed, *arrays),
    )


def project_all(left, weight):
    rows, width = left.shape[0], weight[0][0].shape[1]
    parts, count = lax.axis_size("dp"), lax.axis_size("mp")
    shape = (parts, count // 2, rows // (parts * count), width * len(weight))
    arrays, spec = packed([weight])
    return kernel_call(
        functools.partial(project_kernel, spec),
        (jax.ShapeDtypeStruct(shape, jnp.bfloat16), jax.ShapeDtypeStruct(shape, jnp.float32)),
        (left, *arrays),
        [pltpu.VMEM((rows, width), jnp.float32)],
    )


def conv_kernel(spec, x_ref, before_ref, after_ref, taps_ref, *refs):
    weight = unpacked(spec, refs[:-5])
    sent_ref, kept_ref, product_ref, padded_ref, active_ref = refs[-5:]
    edge, rows = before_ref.shape[0], x_ref.shape[0]
    taps = taps_ref.shape[0]
    shift = edge - taps // 2
    padded_ref[:edge, :] = before_ref[...].astype(jnp.float32)
    padded_ref[edge : edge + rows, :] = x_ref[...].astype(jnp.float32)
    padded_ref[edge + rows :, :] = after_ref[...].astype(jnp.float32)
    block = 64 if rows % 64 == 0 else rows
    for first in range(0, x_ref.shape[1], 128):
        columns = slice(first, first + 128)

        @pl.loop(0, rows // block)
        def _(r):
            base = pl.multiple_of(r * block, block)
            window = padded_ref[pl.ds(base, block + 2 * edge), columns]
            total = jnp.zeros((block, window.shape[1]), jnp.float32)
            for t in range(taps):
                total += taps_ref[t : t + 1, columns] * window[t + shift : t + shift + block]
            active_ref[pl.ds(base, block), columns] = (total / (1.0 + jnp.exp(-total))).astype(
                jnp.bfloat16
            )

    project_refs(active_ref, [weight], sent_ref, kept_ref, product_ref)


def conv_branch(units, taps, blocks, before, after):
    rows, channels = units.shape
    width = blocks[0][0].shape[1]
    arrays, spec = packed(blocks)
    return kernel_call(
        functools.partial(conv_kernel, spec),
        shares(rows, width * len(blocks)),
        (units, before, after, taps, *arrays),
        [
            pltpu.VMEM((rows, width), jnp.float32),
            pltpu.VMEM((rows + 2 * before.shape[0], channels), jnp.float32),
            pltpu.VMEM((rows, channels), jnp.bfloat16),
        ],
    )


def hidden_kernel(spec, halves, mask_ref, *refs):
    weight = unpacked(spec, refs[halves:-2])
    o_ref, x_ref = refs[-2:]
    if halves == 2:
        place_rows(x_ref, refs[0], refs[1])
    else:
        x_ref[...] = refs[0][...]
    rows, width = o_ref.shape
    tile_rows, block = rows // mask_ref.shape[0], width // mask_ref.shape[1]
    tiles, tile = column_tiles(width)

    @pl.loop(0, tiles)
    def _(n):
        units = through(x_ref, weight, pl.ds(pl.multiple_of(n * tile, tile), tile))
        units = units / (1.0 + jnp.exp(-units))
        for r in range(mask_ref.shape[0]):
            for j in range(tile // block):
                masked = (
                    units[r * tile_rows : (r + 1) * tile_rows, j * block : (j + 1) * block]
                    * mask_ref[r, n * (tile // block) + j]
                )
                o_ref[
                    r * tile_rows : (r + 1) * tile_rows,
                    pl.ds(pl.multiple_of(n * tile + j * block, block), block),
                ] = masked.astype(o_ref.dtype)


def hidden_of(rows, weight, mask):
    count = sum(piece.shape[0] for piece in rows)
    arrays, spec = packed(weight)
    return kernel_call(
        functools.partial(hidden_kernel, spec, len(rows)),
        jax.ShapeDtypeStruct((count, arrays[0].shape[1]), jnp.bfloat16),
        (mask, *rows, *arrays),
        [pltpu.VMEM((count, rows[0].shape[1]), jnp.bfloat16)],
        scalars=1,
    )


def on_device(
    residual_in,
    queries,
    keys,
    values,
    w_out,
    conv_value,
    conv_gate,
    depth_kernel,
    conv_out,
    ffn_in,
    ffn_down,
    ffn_mask,
):
    row_count = queries.shape[0]
    count, parts, here = lax.axis_size("seq"), lax.axis_size("dp"), lax.axis_index("dp")
    own_units = ffn_in.shape[1] // parts
    in_columns = lax.dynamic_slice_in_dim(ffn_in, here * own_units, own_units, axis=1)
    down_rows = lax.dynamic_slice_in_dim(ffn_down, here * own_units, own_units, axis=0)
    paired = parts == 2 and lax.axis_size("mp") == 4
    line = Line(3, 1)
    line.add(0, 4, ("w_out", w_out))
    line.add(1, 7, ("value", conv_value), ("gate", conv_gate))
    line.add(3, 8, ("conv_out", conv_out))
    by_head = queries.shape[1] % (count * HEAD_DIM) == 0
    if by_head:
        pieces = heads_by_device(queries, keys, values)
    line.begin()

    share_count = row_count // lax.axis_size("mp")
    stream = lax.dynamic_slice_in_dim(
        residual_in, lax.axis_index("mp") * share_count, share_count, 0
    )
    if by_head:
        pieces, stream = line.visits(2, (pieces, stream))
        weight_in = Gathered(pieces[0], in_columns)
        pieces = attention_by_head(pieces)
        pieces = [pieces[0]] + [
            lax.ppermute(pieces[d], "seq", [(i, (i - d) % count) for i in range(count)])
            for d in range(1, count)
        ]
        pieces = line.visits(1, pieces)
        pieces = line.until(["w_out"], pieces)
        sent, kept = project_heads(pieces, [line.take("w_out")])
    else:
        heads_out = attention(queries, keys, values)
        weight_in = Gathered(heads_out, in_columns)
        heads_out = line.until(["w_out"], heads_out)
        sent, kept = project(heads_out, [line.take("w_out")])
    cut = ffn_down.shape[1] // 2
    downs = [Gathered(kept, down_rows[:, c * cut : (c + 1) * cut]) for c in range(2)]
    kept, taken = fenced(scatter_sum, sent, kept)
    kept, taken = line.visits(2, (kept, taken))
    stream, norm_one = advance(stream, kept, taken, True)
    norm_one = fenced(widen, norm_one)
    norm_one = line.visits(1, norm_one)

    norm_one = line.until(["value", "gate"], norm_one)
    units = gated(norm_one, line.take("value"), line.take("gate"))
    edge = -(-(depth_kernel.shape[0] // 2) // 16) * 16
    up = [(i, i + 1) for i in range(count - 1)]
    before = lax.ppermute(units[row_count - edge :], "seq", up)
    after = lax.ppermute(units[:edge], "seq", [(j, i) for i, j in up])
    units = line.visits(1, units)
    units = line.until(["conv_out"], units)
    sent, kept = conv_branch(units, depth_kernel, line.take("conv_out"), before, after)
    kept, taken = fenced(scatter_sum, sent, kept)
    stream, norm_two = advance(stream, kept, taken, False)

    blocks = ffn_mask.shape[1] // parts
    mask = ffn_mask.astype(jnp.float32)
    if paired:
        rows = rows_of_all(norm_two)
        other = swap(mask, "dp", 1)
        mask = jnp.concatenate(
            [jnp.where(here == 0, mask, other), jnp.where(here == 0, other, mask)], axis=0
        )
    else:
        rows = (lax.all_gather(norm_two, ("dp", "mp"), axis=0, tiled=True),)
        mask = lax.all_gather(mask, "dp", axis=0, tiled=True)
    mask = lax.dynamic_slice_in_dim(mask, here * blocks, blocks, axis=1)
    hidden = hidden_of(rows, weight_in.take(), mask)
    pieces = []
    for down in downs:
        hidden = down.end(hidden)
        sent, kept = project_all(hidden, down.take())
        if paired:
            pieces.append(sum_over_all(sent, kept))
        else:
            mine = lax.axis_index("mp") % 2
            both = [sent.astype(jnp.float32), kept]
            both = jnp.where(mine == 0, jnp.stack(both[::-1], 2), jnp.stack(both, 2))
            pieces.append(
                (
                    lax.psum_scatter(
                        both.reshape(-1, both.shape[-1]).astype(jnp.bfloat16),
                        ("dp", "mp"),
                        scatter_dimension=0,
                        tiled=True,
                    ),
                )
            )
    return finish(stream, pieces)


def solution(mesh):
    in_specs = (
        P(("dp", "seq"), None),
        P(("dp", "seq"), "mp"),
        P(("dp", "seq"), "mp"),
        P(("dp", "seq"), "mp"),
        P("mp", "seq"),
        P("seq", "mp"),
        P("seq", "mp"),
        P(None, "mp"),
        P("mp", "seq"),
        P("seq", "mp"),
        P("mp", "seq"),
        P(("dp", "seq"), "mp"),
    )
    out_specs = P(("dp", "seq", "mp"), None)
    return jax.shard_map(
        on_device, mesh=mesh, in_specs=in_specs, out_specs=out_specs, check_vma=False
    )
```

time: 369 us -> 349 us (0.946)
  waiting for transfers between devices: 225 us -> 174 us
  starting transfers between devices: 47 us -> 79.9 us
  local copies, waits for them, and re-layouts: 37.5 us -> 15.4 us
  between operations: 0.86 us -> 13.6 us
  Pallas kernels: 50.2 us -> 58.7 us
    ppermute x32 -> x33, waiting for transfers between devices: 183 us -> 110 us  [the longest x9 60.3 us: refill(): lax.ppermute(piece, 'seq', ring_pairs('seq'))]
    ppermute x32 -> x33, starting transfers between devices: 18.5 us -> 63.9 us  [the longest x9 38.6 us: refill(): lax.ppermute(piece, 'seq', ring_pairs('seq'))]
    unnamed x137 -> x70, local copies, waits for them, and re-layouts: 20.2 us -> 5.23 us
    ppermute x6 -> x4, waiting for transfers between devices: 13.7 us -> 24.3 us  [scatter_sum(): taken = lax.ppermute(sent, 'mp', xor_pairs(count, bit))]
    ppermute x24 -> x9, starting transfers between devices: 21.7 us -> 11.4 us  [visit(): piece = lax.ppermute(piece, 'dp', ring_pairs('dp'))]
    ppermute x4 -> x2, waiting for transfers between devices: 0.57 us -> 10.2 us  [widen(): taken = lax.ppermute(held, 'mp', xor_pairs(count, bit))]
    pallas_call x7 -> x11, Pallas kernels: 50.2 us -> 58.7 us  [kernel_call(): pl.pallas_call(kernel, out_shape=outs, in_specs=[pl.BlockSpec(memory_spac...]
    all_gather x0 -> x3, waiting for transfers between devices: none -> 8.24 us  [__init__(): self.array = lax.all_gather(array, 'seq', axis=0, tiled=True)]
  transfers between devices with their start and end apart: 66 -> 51, of which waited for: 38 -> 26; matrix products, arithmetic and copies ran while one was open for 9% -> 4% of each run, Pallas kernels for 7% -> 16%
where the time goes in v1:
time: 349 us; the launch traced here: 348 us
  waiting for transfers between devices  174 us (50%)
  starting transfers between devices  79.9 us (23%)
  Pallas kernels  58.7 us (17%)
  local copies, waits for them, and re-layouts  15.4 us (4%)
  between operations  13.6 us (4%)
  other arithmetic  6.06 us (2%)
    ppermute x9, waiting for transfers between devices, refill(): lax.ppermute(piece, 'seq', ring_pairs('seq'))  60.3 us
    pallas_call x11, Pallas kernels, kernel_call(): pl.pallas_call(kernel, out_shape=outs, in_specs=[pl.BlockSpec(memory_spac...  58.7 us
    ppermute x9, starting transfers between devices, refill(): lax.ppermute(piece, 'seq', ring_pairs('seq'))  38.6 us
    ppermute x4, waiting for transfers between devices, scatter_sum(): taken = lax.ppermute(sent, 'mp', xor_pairs(count, bit))  24.3 us
    ppermute x3, waiting for transfers between devices, on_device(): lax.ppermute(pieces[d], 'seq', [(i, (i - d) % count) for i in range(count)])  23.2 us
    ppermute x16, waiting for transfers between devices, swap(): return lax.ppermute(value, axis, xor_pairs(lax.axis_size(axis), bit))  22.2 us
    ppermute x9, waiting for transfers between devices, visit(): piece = lax.ppermute(piece, 'dp', ring_pairs('dp'))  21.4 us
    ppermute x16, starting transfers between devices, swap(): return lax.ppermute(value, axis, xor_pairs(lax.axis_size(axis), bit))  13.4 us
  transfers between devices with their start and end apart: 51, of which 26 were waited for; matrix products, arithmetic and copies ran while one was open for 4% of the time, Pallas kernels for 16%

profile of v1, /device:TPU:0, one launch (start us, length us, event | category | flops | bytes accessed | tf_op | source)
XLA Modules:
  0.0 347.9 jit_solution(8246352557367472654)
XLA Ops:
  23.2 27.3 %collective-permute-done.9.refs_5_ = bf16[256,512]{1,0:T(8,128)(2,1)S(1)} collective-permute-done((bf16[256,512]{1,0:T(8,128)(2,1)}, bf16[256,512]{1,0:T(8,128)(2,1)S(1)}, u32[]{:S(2)}, u32[]{:S(2)}) %collective-permute-start.9) | collective-permute-done | bytes 262176 | tf_op jit(solution)/shard_map/ppermute | solution.py:73
  50.7 12.5 %collective-permute-start.14 = (bf16[256,512]{1,0:T(8,128)(2,1)S(1)}, bf16[256,512]{1,0:T(8,128)(2,1)S(1)}, u32[]{:S(2)}, u32[]{:S(2)}) collective-permute-start(bf16[256,512]{1,0:T(8,128)(2,1)S(1)} %collective-permute-done.9.refs_5_), channel_id=1, source_target_pairs={{0,8},{8,16},{16,24},{24,0},{1,9},{9,17},{17,25},{25,1},{2,10},{10... | collective-permute-start | bytes 786440 | tf_op jit(solution)/shard_map/ppermute | solution.py:73
  65.2 9.4 %shard_map.119 = (bf16[384,128]{1,0:T(8,128)(2,1)}, bf16[384,128]{1,0:T(8,128)(2,1)}, bf16[384,128]{1,0:T(8,128)(2,1)}, bf16[384,128]{1,0:T(8,128)(2,1)}) custom-call(bf16[384,384]{1,0:T(8,128)(2,1)} %get-tuple-element.123.refs_0_, bf16[384,384]{1,0:T(8,128)(2,1)} %collective-permute-done.6.refs_1_, bf16[384,384]{1,0:T(8,128)(2,1)} %collective-permute-done.7.refs_2_, ...), custom_call_target="tpu_custom_call" | custom-call | tf_op jit(solution)/shard_map/pallas_call | solution.py:283
  78.2 6.0 %collective-permute-done.11.refs_1_ = bf16[384,128]{1,0:T(8,128)(2,1)S(1)} collective-permute-done((bf16[384,128]{1,0:T(8,128)(2,1)}, bf16[384,128]{1,0:T(8,128)(2,1)S(1)}, u32[]{:S(2)}, u32[]{:S(2)}) %collective-permute-start.11) | collective-permute-done | bytes 98336 | tf_op jit(solution)/shard_map/ppermute | solution.py:705
  84.2 17.2 %collective-permute-done.12.refs_2_ = bf16[384,128]{1,0:T(8,128)(2,1)S(1)} collective-permute-done((bf16[384,128]{1,0:T(8,128)(2,1)}, bf16[384,128]{1,0:T(8,128)(2,1)S(1)}, u32[]{:S(2)}, u32[]{:S(2)}) %collective-permute-start.12) | collective-permute-done | bytes 98336 | tf_op jit(solution)/shard_map/ppermute | solution.py:705
  104.4 13.1 %collective-permute-done.18.refs_9_ = bf16[256,512]{1,0:T(8,128)(2,1)S(1)} collective-permute-done((bf16[256,512]{1,0:T(8,128)(2,1)S(1)}, bf16[256,512]{1,0:T(8,128)(2,1)S(1)}, u32[]{:S(2)}, u32[]{:S(2)}) %collective-permute-start.18) | collective-permute-done | bytes 262176 | tf_op jit(solution)/shard_map/ppermute | solution.py:73
  128.6 12.1 %collective-permute-start.22 = (bf16[512,512]{1,0:T(8,128)(2,1)S(1)}, bf16[512,512]{1,0:T(8,128)(2,1)S(1)}, u32[]{:S(2)}, u32[]{:S(2)}) collective-permute-start(bf16[512,512]{1,0:T(8,128)(2,1)S(1)} %collective-permute-done.10.refs_1_), channel_id=1, source_target_pairs={{0,8},{8,16},{16,24},{24,0},{1,9},{9,17},{17,25},{25,1},{2,10},{10... | collective-permute-start | bytes 1572872 | tf_op jit(solution)/shard_map/ppermute | solution.py:73
  140.7 16.1 %conditional.3 = (f32[96,2048]{1,0:T(8,128)S(1)}, bf16[96,2048]{1,0:T(8,128)(2,1)}) conditional(s32[]{:T(128)} %convert_element_type.54, () %tuple.53, (bf16[2,96,2048]{2,1,0:T(8,128)(2,1)S(1)}, f32[2,96,2048]{2,1,0:T(8,128)}) %shard_map.120), branch_computations={%region_0.0_spmd, %region_1.2_spmd} | conditional | flops 786468 | bytes 11010523 | solution.py:194
  146.9 10.0 %collective-permute-done.1 = bf16[1,96,2048]{2,1,0:T(8,128)(2,1)} collective-permute-done((bf16[1,96,2048]{2,1,0:T(8,128)(2,1)}, bf16[1,96,2048]{2,1,0:T(8,128)(2,1)}, u32[]{:S(2)}, u32[]{:S(2)}) %collective-permute-start.1) | collective-permute-done | bytes 393248 | tf_op jit(solution)/shard_map/cond/branch_1_fun/ppermute | solution.py:207
  156.9 6.6 %collective-permute-done.22.refs_3_ = bf16[512,512]{1,0:T(8,128)(2,1)S(1)} collective-permute-done((bf16[512,512]{1,0:T(8,128)(2,1)S(1)}, bf16[512,512]{1,0:T(8,128)(2,1)S(1)}, u32[]{:S(2)}, u32[]{:S(2)}) %collective-permute-start.22) | collective-permute-done | bytes 524320 | tf_op jit(solution)/shard_map/ppermute | solution.py:73
  163.5 6.0 %collective-permute-start.24 = (bf16[512,512]{1,0:T(8,128)(2,1)S(1)}, bf16[512,512]{1,0:T(8,128)(2,1)S(1)}, u32[]{:S(2)}, u32[]{:S(2)}) collective-permute-start(bf16[512,512]{1,0:T(8,128)(2,1)S(1)} %collective-permute-done.22.refs_3_), channel_id=1, source_target_pairs={{0,8},{8,16},{16,24},{24,0},{1,9},{9,17},{17,25},{25,1},{2,10},{10... | collective-permute-start | bytes 1572872 | tf_op jit(solution)/shard_map/ppermute | solution.py:73
  173.8 13.3 %collective-permute-done.23.refs_3_ = bf16[256,512]{1,0:T(8,128)(2,1)} collective-permute-done((bf16[256,512]{1,0:T(8,128)(2,1)}, bf16[256,512]{1,0:T(8,128)(2,1)}, u32[]{:S(2)}, u32[]{:S(2)}) %collective-permute-start.23) | collective-permute-done | bytes 262176 | tf_op jit(solution)/shard_map/ppermute | solution.py:73
  189.4 13.4 %conditional.4 = (bf16[384,2048]{1,0:T(8,128)(2,1)S(1)}) conditional(s32[]{:T(128)} %convert_element_type.54, () %tuple.67, bf16[96,2048]{1,0:T(8,128)(2,1)} %get-tuple-element.171), branch_computations={%region_2.3_spmd, %region_3.4_spmd} | conditional | flops 2752547 | bytes 17301940 | solution.py:194
  190.9 8.0 %collective-permute-done.2 = bf16[1,96,2048]{2,1,0:T(8,128)(2,1)S(1)} collective-permute-done((bf16[1,96,2048]{2,1,0:T(8,128)(2,1)}, bf16[1,96,2048]{2,1,0:T(8,128)(2,1)S(1)}, u32[]{:S(2)}, u32[]{:S(2)}) %collective-permute-start.2) | collective-permute-done | bytes 393248 | tf_op jit(solution)/shard_map/cond/branch_1_fun/ppermute | solution.py:225
  205.9 16.6 %collective-permute-done.26.refs_4_ = bf16[256,512]{1,0:T(8,128)(2,1)S(1)} collective-permute-done((bf16[256,512]{1,0:T(8,128)(2,1)}, bf16[256,512]{1,0:T(8,128)(2,1)S(1)}, u32[]{:S(2)}, u32[]{:S(2)}) %collective-permute-start.26) | collective-permute-done | bytes 262176 | tf_op jit(solution)/shard_map/ppermute | solution.py:92
  223.3 4.9 %shard_map.122.x_ref = bf16[384,512]{1,0:T(8,128)(2,1)} custom-call(bf16[384,2048]{1,0:T(8,128)(2,1)S(1)} %get-tuple-element.237.x_ref, bf16[512,512]{1,0:T(8,128)(2,1)} %refs_0_.2, bf16[512,512]{1,0:T(8,128)(2,1)} %copy-done.8, bf16[512,512]{1,0:T(8,128)(2,1)} %copy-done.9, bf16[512,512]{1,0:T(8,128)(2,1)} %copy-done.10, ...), custom_call_target="tpu_custom_call" | custom-call | tf_op jit(solution)/shard_map/pallas_call | solution.py:283
  240.8 9.4 %shard_map.123 = (bf16[2,96,2048]{2,1,0:T(8,128)(2,1)S(1)}, f32[2,96,2048]{2,1,0:T(8,128)}) custom-call(bf16[384,512]{1,0:T(8,128)(2,1)} %shard_map.122.x_ref, bf16[16,512]{1,0:T(8,128)(2,1)} %copy-done.30, bf16[16,512]{1,0:T(8,128)(2,1)} %copy-done.31, f32[31,512]{1,0:T(8,128)} %taps_ref.1, bf16[512,512]{1,0:T(8,128)(2,1)} %refs_0_.3, ...), custom_call_target="tpu_custom_call" | custom-call | tf_op jit(solution)/shard_map/pallas_call | solution.py:283
  250.2 15.3 %conditional.5 = (f32[96,2048]{1,0:T(8,128)S(1)}, bf16[96,2048]{1,0:T(8,128)(2,1)}) conditional(s32[]{:T(128)} %convert_element_type.54, () %tuple.66, (bf16[2,96,2048]{2,1,0:T(8,128)(2,1)S(1)}, f32[2,96,2048]{2,1,0:T(8,128)}) %shard_map.123), branch_computations={%region_4.5_spmd, %region_5.6_spmd} | conditional | flops 786468 | bytes 11010523 | solution.py:194
  255.7 9.8 %collective-permute-done.5 = bf16[1,96,2048]{2,1,0:T(8,128)(2,1)} collective-permute-done((bf16[1,96,2048]{2,1,0:T(8,128)(2,1)S(1)}, bf16[1,96,2048]{2,1,0:T(8,128)(2,1)}, u32[]{:S(2)}, u32[]{:S(2)}) %collective-permute-start.5) | collective-permute-done | bytes 393248 | tf_op jit(solution)/shard_map/cond/branch_1_fun/ppermute | solution.py:207
  270.4 7.9 %collective-permute-done.34 = bf16[96,2048]{1,0:T(8,128)(2,1)S(1)} collective-permute-done((bf16[96,2048]{1,0:T(8,128)(2,1)}, bf16[96,2048]{1,0:T(8,128)(2,1)S(1)}, u32[]{:S(2)}, u32[]{:S(2)}) %collective-permute-start.34) | collective-permute-done | bytes 393248 | tf_op jit(solution)/shard_map/ppermute | solution.py:235
  291.2 8.9 %shard_map.125.left_ref = bf16[768,1024]{1,0:T(8,128)(2,1)} custom-call(f32[6,8]{1,0:T(8,128)} %constant_dynamic-slice_fusion.2.mask_ref, bf16[384,2048]{1,0:T(8,128)(2,1)} %copy-done.2, bf16[384,2048]{1,0:T(8,128)(2,1)} %copy-done.5, bf16[2048,1024]{1,0:T(8,128)(2,1)} %all-gather.4.cloned.1.call-done.refs_2_), custom_call_target="tpu_custom_call" | custom-call | tf_op jit(solution)/shard_map/pallas_call | solution.py:283
  300.1 5.9 %shard_map.126 = (bf16[2,2,96,1024]{3,2,1,0:T(8,128)(2,1)}, f32[2,2,96,1024]{3,2,1,0:T(8,128)}) custom-call(bf16[768,1024]{1,0:T(8,128)(2,1)} %shard_map.125.left_ref, bf16[4096,256]{1,0:T(8,128)(2,1)} %all-gather.6.cloned.1.call-done.refs_0_), custom_call_target="tpu_custom_call" | custom-call | tf_op jit(solution)/shard_map/pallas_call | solution.py:283
  305.9 8.2 %all-gather.8.cloned.1.call-done.refs_0_ = bf16[4096,256]{1,0:T(8,128)(2,1)} async-done(((bf16[1024,256]{1,0:T(8,128)(2,1)}), bf16[4096,256]{1,0:T(8,128)(2,1)}) %all-gather.8.cloned.1.call-update) | async-done | bytes 2097168 | tf_op jit(solution)/shard_map/all_gather | solution.py:144
  314.2 5.9 %shard_map.127 = (bf16[2,2,96,1024]{3,2,1,0:T(8,128)(2,1)}, f32[2,2,96,1024]{3,2,1,0:T(8,128)}) custom-call(bf16[768,1024]{1,0:T(8,128)(2,1)} %shard_map.125.left_ref, bf16[4096,256]{1,0:T(8,128)(2,1)} %all-gather.8.cloned.1.call-done.refs_0_), custom_call_target="tpu_custom_call" | custom-call | tf_op jit(solution)/shard_map/pallas_call | solution.py:283
  (207 shorter events, 115.3 us)
Async XLA Ops:
  6.5 283.5 %all-gather.4.cloned.1.call-start = ((), (), s32[]{:S(2)}) async-start(), calls=%async_computation | async-start | bytes 5242880 | tf_op jit(solution)/shard_map/all_gather | solution.py:144
  8.6 42.0 %collective-permute-start.10 = (bf16[512,512]{1,0:T(8,128)(2,1)}, bf16[512,512]{1,0:T(8,128)(2,1)S(1)}, u32[]{:S(2)}, u32[]{:S(2)}) collective-permute-start(bf16[512,512]{1,0:T(8,128)(2,1)} %pad_maximum_fusion.1), channel_id=1, source_target_pairs={{0,8},{8,16},{16,24},{24,0},{1,9},{9,17},{17,25},{25,1},{2,10},{10... | collective-permute-start | bytes 1572872 | tf_op jit(solution)/shard_map/ppermute | solution.py:73
  14.1 36.5 %collective-permute-start.6 = (bf16[384,384]{1,0:T(8,128)(2,1)}, bf16[384,384]{1,0:T(8,128)(2,1)}, u32[]{:S(2)}, u32[]{:S(2)}) collective-permute-start(bf16[384,384]{1,0:T(8,128)(2,1)} %get-tuple-element.114), channel_id=1, source_target_pairs={{0,8},{8,16},{16,24},{24,0},{1,9},{9,17},{17,25},{25,1},{2,10},{10... | collective-permute-start | bytes 884744 | tf_op jit(solution)/shard_map/ppermute | solution.py:504
  15.7 34.9 %collective-permute-start.7 = (bf16[384,384]{1,0:T(8,128)(2,1)}, bf16[384,384]{1,0:T(8,128)(2,1)}, u32[]{:S(2)}, u32[]{:S(2)}) collective-permute-start(bf16[384,384]{1,0:T(8,128)(2,1)} %get-tuple-element.115), channel_id=1, source_target_pairs={{0,16},{8,24},{16,0},{24,8},{1,17},{9,25},{17,1},{25,9},{2,18},{10... | collective-permute-start | bytes 884744 | tf_op jit(solution)/shard_map/ppermute | solution.py:504
  16.7 33.9 %collective-permute-start.8 = (bf16[384,384]{1,0:T(8,128)(2,1)}, bf16[384,384]{1,0:T(8,128)(2,1)}, u32[]{:S(2)}, u32[]{:S(2)}) collective-permute-start(bf16[384,384]{1,0:T(8,128)(2,1)} %get-tuple-element.116), channel_id=1, source_target_pairs={{0,24},{8,0},{16,8},{24,16},{1,25},{9,1},{17,9},{25,17},{2,26},{10... | collective-permute-start | bytes 884744 | tf_op jit(solution)/shard_map/ppermute | solution.py:504
  20.3 30.2 %collective-permute-start.9 = (bf16[256,512]{1,0:T(8,128)(2,1)}, bf16[256,512]{1,0:T(8,128)(2,1)S(1)}, u32[]{:S(2)}, u32[]{:S(2)}) collective-permute-start(bf16[256,512]{1,0:T(8,128)(2,1)} %constant_dynamic-slice_fusion.6), channel_id=1, source_target_pairs={{0,8},{8,16},{16,24},{24,0},{1,9},{9,17},{17,25},{25,1},{2,10},{10... | collective-permute-start | bytes 786440 | tf_op jit(solution)/shard_map/ppermute | solution.py:73
  50.6 249.5 %all-gather.6.cloned.1.call-start = ((), (), s32[]{:S(2)}) async-start(), calls=%async_computation.1 | async-start | bytes 2621440 | tf_op jit(solution)/shard_map/all_gather | solution.py:144
  50.7 25.5 %collective-permute-start.14 = (bf16[256,512]{1,0:T(8,128)(2,1)S(1)}, bf16[256,512]{1,0:T(8,128)(2,1)S(1)}, u32[]{:S(2)}, u32[]{:S(2)}) collective-permute-start(bf16[256,512]{1,0:T(8,128)(2,1)S(1)} %collective-permute-done.9.refs_5_), channel_id=1, source_target_pairs={{0,8},{8,16},{16,24},{24,0},{1,9},{9,17},{17,25},{25,1},{2,10},{10... | collective-permute-start | bytes 786440 | tf_op jit(solution)/shard_map/ppermute | solution.py:73
  64.6 38.5 %collective-permute-start.17 = (bf16[512,512]{1,0:T(8,128)(2,1)S(1)}, bf16[512,512]{1,0:T(8,128)(2,1)S(1)}, u32[]{:S(2)}, u32[]{:S(2)}) collective-permute-start(bf16[512,512]{1,0:T(8,128)(2,1)S(1)} %collective-permute-done.10.refs_1_), channel_id=1, source_target_pairs={{0,1},{1,0},{2,3},{3,2},{4,5},{5,4},{6,7},{7,6},{8,9},{9,8},{10,11... | collective-permute-start | bytes 1572872 | tf_op jit(solution)/shard_map/ppermute | solution.py:92
  74.6 26.8 %collective-permute-start.12 = (bf16[384,128]{1,0:T(8,128)(2,1)}, bf16[384,128]{1,0:T(8,128)(2,1)S(1)}, u32[]{:S(2)}, u32[]{:S(2)}) collective-permute-start(bf16[384,128]{1,0:T(8,128)(2,1)} %get-tuple-element.129), channel_id=1, source_target_pairs={{0,16},{8,24},{16,0},{24,8},{1,17},{9,25},{17,1},{25,9},{2,18},{10... | collective-permute-start | bytes 294920 | tf_op jit(solution)/shard_map/ppermute | solution.py:705
  76.1 25.3 %collective-permute-start.13 = (bf16[384,128]{1,0:T(8,128)(2,1)}, bf16[384,128]{1,0:T(8,128)(2,1)S(1)}, u32[]{:S(2)}, u32[]{:S(2)}) collective-permute-start(bf16[384,128]{1,0:T(8,128)(2,1)} %get-tuple-element.130), channel_id=1, source_target_pairs={{0,8},{8,16},{16,24},{24,0},{1,9},{9,17},{17,25},{25,1},{2,10},{10... | collective-permute-start | bytes 294920 | tf_op jit(solution)/shard_map/ppermute | solution.py:705
  76.7 26.3 %collective-permute-start.16 = (bf16[256,512]{1,0:T(8,128)(2,1)S(1)}, bf16[256,512]{1,0:T(8,128)(2,1)}, u32[]{:S(2)}, u32[]{:S(2)}) collective-permute-start(bf16[256,512]{1,0:T(8,128)(2,1)S(1)} %constant_dynamic-slice_fusion.3), channel_id=1, source_target_pairs={{0,8},{8,16},{16,24},{24,0},{1,9},{9,17},{17,25},{25,1},{2,10},{10... | collective-permute-start | bytes 786440 | tf_op jit(solution)/shard_map/ppermute | solution.py:73
  101.5 16.1 %collective-permute-start.18 = (bf16[256,512]{1,0:T(8,128)(2,1)S(1)}, bf16[256,512]{1,0:T(8,128)(2,1)S(1)}, u32[]{:S(2)}, u32[]{:S(2)}) collective-permute-start(bf16[256,512]{1,0:T(8,128)(2,1)S(1)} %collective-permute-done.14.refs_7_), channel_id=1, source_target_pairs={{0,8},{8,16},{16,24},{24,0},{1,9},{9,17},{17,25},{25,1},{2,10},{10... | collective-permute-start | bytes 786440 | tf_op jit(solution)/shard_map/ppermute | solution.py:73
  101.5 16.0 %collective-permute-start.19 = (bf16[256,512]{1,0:T(8,128)(2,1)S(1)}, bf16[256,512]{1,0:T(8,128)(2,1)S(1)}, u32[]{:S(2)}, u32[]{:S(2)}) collective-permute-start(bf16[256,512]{1,0:T(8,128)(2,1)S(1)} %collective-permute-done.14.refs_7_), channel_id=1, source_target_pairs={{0,1},{1,0},{2,3},{3,2},{4,5},{5,4},{6,7},{7,6},{8,9},{9,8},{10,11... | collective-permute-start | bytes 786440 | tf_op jit(solution)/shard_map/ppermute | solution.py:92
  103.9 16.3 %collective-permute-start.20 = (bf16[256,512]{1,0:T(8,128)(2,1)}, bf16[256,512]{1,0:T(8,128)(2,1)S(1)}, u32[]{:S(2)}, u32[]{:S(2)}) collective-permute-start(bf16[256,512]{1,0:T(8,128)(2,1)} %collective-permute-done.16.refs_1_), channel_id=1, source_target_pairs={{0,1},{1,0},{2,3},{3,2},{4,5},{5,4},{6,7},{7,6},{8,9},{9,8},{10,11... | collective-permute-start | bytes 786440 | tf_op jit(solution)/shard_map/ppermute | solution.py:92
  128.6 185.6 %all-gather.8.cloned.1.call-start = ((), (), s32[]{:S(2)}) async-start(), calls=%async_computation.2 | async-start | bytes 2621440 | tf_op jit(solution)/shard_map/all_gather | solution.py:144
  128.6 34.8 %collective-permute-start.22 = (bf16[512,512]{1,0:T(8,128)(2,1)S(1)}, bf16[512,512]{1,0:T(8,128)(2,1)S(1)}, u32[]{:S(2)}, u32[]{:S(2)}) collective-permute-start(bf16[512,512]{1,0:T(8,128)(2,1)S(1)} %collective-permute-done.10.refs_1_), channel_id=1, source_target_pairs={{0,8},{8,16},{16,24},{24,0},{1,9},{9,17},{17,25},{25,1},{2,10},{10... | collective-permute-start | bytes 1572872 | tf_op jit(solution)/shard_map/ppermute | solution.py:73
  163.5 39.3 %collective-permute-start.24 = (bf16[512,512]{1,0:T(8,128)(2,1)S(1)}, bf16[512,512]{1,0:T(8,128)(2,1)S(1)}, u32[]{:S(2)}, u32[]{:S(2)}) collective-permute-start(bf16[512,512]{1,0:T(8,128)(2,1)S(1)} %collective-permute-done.22.refs_3_), channel_id=1, source_target_pairs={{0,8},{8,16},{16,24},{24,0},{1,9},{9,17},{17,25},{25,1},{2,10},{10... | collective-permute-start | bytes 1572872 | tf_op jit(solution)/shard_map/ppermute | solution.py:73
  169.5 33.3 %collective-permute-start.25 = (bf16[512,512]{1,0:T(8,128)(2,1)S(1)}, bf16[512,512]{1,0:T(8,128)(2,1)}, u32[]{:S(2)}, u32[]{:S(2)}) collective-permute-start(bf16[512,512]{1,0:T(8,128)(2,1)S(1)} %collective-permute-done.22.refs_3_), channel_id=1, source_target_pairs={{0,1},{1,0},{2,3},{3,2},{4,5},{5,4},{6,7},{7,6},{8,9},{9,8},{10,11... | collective-permute-start | bytes 1572872 | tf_op jit(solution)/shard_map/ppermute | solution.py:92
  171.3 15.8 %collective-permute-start.23 = (bf16[256,512]{1,0:T(8,128)(2,1)}, bf16[256,512]{1,0:T(8,128)(2,1)}, u32[]{:S(2)}, u32[]{:S(2)}) collective-permute-start(bf16[256,512]{1,0:T(8,128)(2,1)} %collective-permute-done.16.refs_1_), channel_id=1, source_target_pairs={{0,8},{8,16},{16,24},{24,0},{1,9},{9,17},{17,25},{25,1},{2,10},{10... | collective-permute-start | bytes 786440 | tf_op jit(solution)/shard_map/ppermute | solution.py:73
  202.8 19.7 %collective-permute-start.27 = (bf16[512,512]{1,0:T(8,128)(2,1)S(1)}, bf16[512,512]{1,0:T(8,128)(2,1)S(1)}, u32[]{:S(2)}, u32[]{:S(2)}) collective-permute-start(bf16[512,512]{1,0:T(8,128)(2,1)S(1)} %collective-permute-done.24.refs_5_), channel_id=1, source_target_pairs={{0,1},{1,0},{2,3},{3,2},{4,5},{5,4},{6,7},{7,6},{8,9},{9,8},{10,11... | collective-permute-start | bytes 1572872 | tf_op jit(solution)/shard_map/ppermute | solution.py:92
  204.6 17.8 %collective-permute-start.26 = (bf16[256,512]{1,0:T(8,128)(2,1)}, bf16[256,512]{1,0:T(8,128)(2,1)S(1)}, u32[]{:S(2)}, u32[]{:S(2)}) collective-permute-start(bf16[256,512]{1,0:T(8,128)(2,1)} %collective-permute-done.23.refs_3_), channel_id=1, source_target_pairs={{0,1},{1,0},{2,3},{3,2},{4,5},{5,4},{6,7},{7,6},{8,9},{9,8},{10,11... | collective-permute-start | bytes 786440 | tf_op jit(solution)/shard_map/ppermute | solution.py:92
  204.9 23.4 %collective-permute-start.28 = (bf16[256,512]{1,0:T(8,128)(2,1)}, bf16[256,512]{1,0:T(8,128)(2,1)S(1)}, u32[]{:S(2)}, u32[]{:S(2)}) collective-permute-start(bf16[256,512]{1,0:T(8,128)(2,1)} %collective-permute-done.23.refs_3_), channel_id=1, source_target_pairs={{0,8},{8,16},{16,24},{24,0},{1,9},{9,17},{17,25},{25,1},{2,10},{10... | collective-permute-start | bytes 786440 | tf_op jit(solution)/shard_map/ppermute | solution.py:73
  305.9 14.2 %collective-permute-start.38 = (bf16[2,2,96,1024]{3,2,1,0:T(8,128)(2,1)}, bf16[2,2,96,1024]{3,2,1,0:T(8,128)(2,1)S(1)}, u32[]{:S(2)}, u32[]{:S(2)}) collective-permute-start(bf16[2,2,96,1024]{3,2,1,0:T(8,128)(2,1)} %get-tuple-element.199), channel_id=1, source_target_pairs={{0,2},{2,0},{4,6},{6,4},{1,3},{3,1},{5,7},{7,5},{8,10},{10,8},{12,... | collective-permute-start | bytes 2359304 | tf_op jit(solution)/shard_map/ppermute | solution.py:235
  (60 other events, 804.0 us)
Sparse Core Ops, SparseCore 0:
  50.7 138.1 all-gather.3
  190.5 49.8 all-gather.5
  269.5 44.6 all-gather.7

commit v2 on v1

--- a/solution.py
+++ b/solution.py
@@ -37,14 +37,15 @@
     def __init__(self, depth, lag):
         self.depth, self.lag = depth, lag
         self.waiting, self.under_way, self.crossing = [], [], []
-        self.parts, self.pieces, self.token = {}, {}, None
-
-    def add(self, first, last, *stream):
+        self.parts, self.pieces, self.needed, self.token = {}, {}, {}, None
+
+    def add(self, first, last, *stream, shared=True):
         by_width = {}
         for name, array in stream:
             self.parts[name, 0] = [Rows(array, 0, array.shape[0])]
+            self.needed[name] = lax.axis_size("dp") if shared else 1
             by_width.setdefault(array.shape[1], []).append((name, array))
-        count, here = lax.axis_size("dp"), lax.axis_index("dp")
+        count, here = lax.axis_size("dp") if shared else 1, lax.axis_index("dp") if shared else 0
         steps = lax.axis_size("seq") - 1
         for held in by_width.values():
             fields = tuple((name, array.shape[0] // count) for name, array in held)
@@ -88,7 +89,7 @@
             self.token = self.pieces[fields, t] = piece
             self.note(fields, t, piece)
             self.refill()
-            for _ in range(1, lax.axis_size("dp")):
+            for _ in range(1, self.needed[fields[0][0]]):
                 piece = lax.ppermute(piece, "dp", ring_pairs("dp"))
                 self.crossing.append((fields, t, piece))
         else:
@@ -111,7 +112,7 @@
     def until(self, names, beside, first=0, last=None):
         last = lax.axis_size("seq") if last is None else last
         wanted = [(name, t) for name in names for t in range(max(first, 1), last)]
-        while any(len(self.parts.get(key, ())) < lax.axis_size("dp") for key in wanted):
+        while any(len(self.parts.get(key, ())) < self.needed[key[0]] for key in wanted):
             arrived = all(key in self.parts for key in wanted)
             beside = self.cross(beside) if arrived else self.visit(beside)
         return beside
@@ -137,17 +138,39 @@
 
 
 class Gathered:
-    def __init__(self, token, array):
-        self.rows = array.shape[0]
+    def __init__(self, token, array, shared=False):
+        self.rows, axes, self.other = array.shape[0], "seq", None
+        self.cut = shared == "cross" and self.rows % (128 * lax.axis_size("dp")) == 0
+        if shared:
+            rows = self.rows // lax.axis_size("dp")
+            axes = "seq" if self.cut else ("seq", "dp")
+            array = lax.dynamic_slice_in_dim(array, lax.axis_index("dp") * rows, rows, axis=0)
         if token is not None:
             array, _ = lax.optimization_barrier((array, token))
-        self.array = lax.all_gather(array, "seq", axis=0, tiled=True)
+        self.array = lax.all_gather(array, axes, axis=0, tiled=True)
+
+    def cross(self, beside):
+        if self.cut:
+            beside, self.array = lax.optimization_barrier((beside, self.array))
+            self.other = [self.array]
+            for _ in range(1, lax.axis_size("dp")):
+                self.other.append(lax.ppermute(self.other[-1], "dp", ring_pairs("dp")))
+        return beside
 
     def end(self, beside):
-        beside, self.array = lax.optimization_barrier((beside, self.array))
+        if self.cut:
+            beside, self.other = lax.optimization_barrier((beside, self.other))
+        else:
+            beside, self.array = lax.optimization_barrier((beside, self.array))
         return beside
 
     def take(self):
+        if self.cut:
+            rows = self.rows // len(self.other)
+            return [
+                [Rows(part, 0, rows, (t, rows)) for part in self.other]
+                for t in range(lax.axis_size("seq"))
+            ]
         return [
             [Rows(self.array, 0, self.rows, (t, self.rows))] for t in range(lax.axis_size("seq"))
         ]
@@ -685,36 +708,38 @@
     down_rows = lax.dynamic_slice_in_dim(ffn_down, here * own_units, own_units, axis=0)
     paired = parts == 2 and lax.axis_size("mp") == 4
     line = Line(3, 1)
-    line.add(0, 4, ("w_out", w_out))
-    line.add(1, 7, ("value", conv_value), ("gate", conv_gate))
-    line.add(3, 8, ("conv_out", conv_out))
+    line.add(0, 4, ("value", conv_value), ("gate", conv_gate))
+    line.add(1, 5, ("conv_out", conv_out))
     by_head = queries.shape[1] % (count * HEAD_DIM) == 0
     if by_head:
         pieces = heads_by_device(queries, keys, values)
+    wide = ffn_down.shape[1]
+    last = 128 if wide % (2 * 128) == 0 else wide // 2
+    line.add(6, 8, ("down", down_rows[:, wide - last :]), shared=False)
     line.begin()
+    weight_out = Gathered(None, w_out, True)
 
     share_count = row_count // lax.axis_size("mp")
     stream = lax.dynamic_slice_in_dim(
         residual_in, lax.axis_index("mp") * share_count, share_count, 0
     )
+    weight_in = Gathered(None, in_columns)
     if by_head:
-        pieces, stream = line.visits(2, (pieces, stream))
-        weight_in = Gathered(pieces[0], in_columns)
+        pieces, stream = line.visits(1, (pieces, stream))
+        pieces = weight_out.cross(pieces)
         pieces = attention_by_head(pieces)
         pieces = [pieces[0]] + [
             lax.ppermute(pieces[d], "seq", [(i, (i - d) % count) for i in range(count)])
             for d in range(1, count)
         ]
-        pieces = line.visits(1, pieces)
-        pieces = line.until(["w_out"], pieces)
-        sent, kept = project_heads(pieces, [line.take("w_out")])
+        pieces = line.visits(2, pieces)
+        pieces = weight_out.end(pieces)
+        sent, kept = project_heads(pieces, [weight_out.take()])
     else:
         heads_out = attention(queries, keys, values)
-        weight_in = Gathered(heads_out, in_columns)
-        heads_out = line.until(["w_out"], heads_out)
-        sent, kept = project(heads_out, [line.take("w_out")])
-    cut = ffn_down.shape[1] // 2
-    downs = [Gathered(kept, down_rows[:, c * cut : (c + 1) * cut]) for c in range(2)]
+        heads_out = weight_out.end(weight_out.cross(heads_out))
+        sent, kept = project(heads_out, [weight_out.take()])
+    downs = [Gathered(kept, down_rows[:, : wide - last])]
     kept, taken = fenced(scatter_sum, sent, kept)
     kept, taken = line.visits(2, (kept, taken))
     stream, norm_one = advance(stream, kept, taken, True)
@@ -727,10 +752,11 @@
     up = [(i, i + 1) for i in range(count - 1)]
     before = lax.ppermute(units[row_count - edge :], "seq", up)
     after = lax.ppermute(units[:edge], "seq", [(j, i) for i, j in up])
-    units = line.visits(1, units)
+    units = line.visits(0, units)
     units = line.until(["conv_out"], units)
     sent, kept = conv_branch(units, depth_kernel, line.take("conv_out"), before, after)
     kept, taken = fenced(scatter_sum, sent, kept)
+    kept, taken = line.visits(2, (kept, taken))
     stream, norm_two = advance(stream, kept, taken, False)
 
     blocks = ffn_mask.shape[1] // parts
@@ -745,11 +771,20 @@
         rows = (lax.all_gather(norm_two, ("dp", "mp"), axis=0, tiled=True),)
         mask = lax.all_gather(mask, "dp", axis=0, tiled=True)
     mask = lax.dynamic_slice_in_dim(mask, here * blocks, blocks, axis=1)
+    rows = line.visits(0, rows)
     hidden = hidden_of(rows, weight_in.take(), mask)
+    hidden = line.visits(0, hidden)
     pieces = []
-    for down in downs:
-        hidden = down.end(hidden)
-        sent, kept = project_all(hidden, down.take())
+    for down in [None, *downs]:
+        if down is None:
+            hidden = line.until(["down"], hidden)
+            sent, kept = project_all(hidden, line.take("down"))
+        else:
+            if pieces and paired:
+                hidden, pieces[-1] = down.end((hidden, pieces[-1]))
+            else:
+                hidden = down.end(hidden)
+            sent, kept = project_all(hidden, down.take())
         if paired:
             pieces.append(sum_over_all(sent, kept))
         else:
@@ -766,7 +801,7 @@
                     ),
                 )
             )
-    return finish(stream, pieces)
+    return finish(stream, [*pieces[1:], pieces[0]])
 
 
 def solution(mesh):

time: 349 us -> 319 us (0.914)
  waiting for transfers between devices: 174 us -> 149 us
  starting transfers between devices: 79.9 us -> 71.6 us
    ppermute x3, waiting for transfers between devices: 0.01 us -> 31.7 us  [heads_by_device(): lax.ppermute(pieces[d], 'seq', [(i, (i + d) % count) for i in range(count)])]
    ppermute x9, waiting for transfers between devices: 60.3 us -> 32.5 us  [refill(): lax.ppermute(piece, 'seq', ring_pairs('seq'))]
    ppermute x9 -> x6, waiting for transfers between devices: 21.4 us -> 0.02 us  [visit(): piece = lax.ppermute(piece, 'dp', ring_pairs('dp'))]
    ppermute x3, waiting for transfers between devices: 23.2 us -> 8.21 us  [on_device(): lax.ppermute(pieces[d], 'seq', [(i, (i - d) % count) for i in range(count)])]
    ppermute x9, starting transfers between devices: 38.6 us -> 29.1 us  [refill(): lax.ppermute(piece, 'seq', ring_pairs('seq'))]
    ppermute x16, waiting for transfers between devices: 22.2 us -> 28.7 us  [swap(): return lax.ppermute(value, axis, xor_pairs(lax.axis_size(axis), bit))]
    ppermute x9 -> x6, starting transfers between devices: 11.4 us -> 5.53 us  [visit(): piece = lax.ppermute(piece, 'dp', ring_pairs('dp'))]
    ppermute x16, starting transfers between devices: 13.4 us -> 17.1 us  [swap(): return lax.ppermute(value, axis, xor_pairs(lax.axis_size(axis), bit))]
  transfers between devices with their start and end apart: 51 -> 48, of which waited for: 26 -> 29; matrix products, arithmetic and copies ran while one was open for 4% -> 5% of each run, Pallas kernels for 16% -> 15%
where the time goes in v2:
time: 319 us; the launch traced here: 318 us
  waiting for transfers between devices  149 us (47%)
  starting transfers between devices  71.6 us (22%)
  Pallas kernels  60.5 us (19%)
  local copies, waits for them, and re-layouts  16.3 us (5%)
  between operations  13.5 us (4%)
  other arithmetic  6.98 us (2%)
    pallas_call x11, Pallas kernels, kernel_call(): pl.pallas_call(kernel, out_shape=outs, in_specs=[pl.BlockSpec(memory_spac...  60.5 us
    ppermute x9, waiting for transfers between devices, refill(): lax.ppermute(piece, 'seq', ring_pairs('seq'))  32.5 us
    ppermute x3, waiting for transfers between devices, heads_by_device(): lax.ppermute(pieces[d], 'seq', [(i, (i + d) % count) for i in range(count)])  31.7 us
    ppermute x9, starting transfers between devices, refill(): lax.ppermute(piece, 'seq', ring_pairs('seq'))  29.1 us
    ppermute x16, waiting for transfers between devices, swap(): return lax.ppermute(value, axis, xor_pairs(lax.axis_size(axis), bit))  28.7 us
    ppermute x4, waiting for transfers between devices, scatter_sum(): taken = lax.ppermute(sent, 'mp', xor_pairs(count, bit))  24.2 us
    ppermute x16, starting transfers between devices, swap(): return lax.ppermute(value, axis, xor_pairs(lax.axis_size(axis), bit))  17.1 us
    all_gather x3, waiting for transfers between devices, __init__(): self.array = lax.all_gather(array, axes, axis=0, tiled=True)  10.6 us
  transfers between devices with their start and end apart: 48, of which 29 were waited for; matrix products, arithmetic and copies ran while one was open for 5% of the time, Pallas kernels for 15%

profile of v2, /device:TPU:0, one launch (start us, length us, event | category | flops | bytes accessed | tf_op | source)
XLA Modules:
  0.0 318.2 jit_solution(209481672138341579)
XLA Ops:
  23.0 19.8 %collective-permute-done.6.refs_1_ = bf16[384,384]{1,0:T(8,128)(2,1)S(1)} collective-permute-done((bf16[384,384]{1,0:T(8,128)(2,1)}, bf16[384,384]{1,0:T(8,128)(2,1)S(1)}, u32[]{:S(2)}, u32[]{:S(2)}) %collective-permute-start.6) | collective-permute-done | bytes 294944 | tf_op jit(solution)/shard_map/ppermute | solution.py:527
  42.8 11.9 %collective-permute-done.7.refs_2_ = bf16[384,384]{1,0:T(8,128)(2,1)S(1)} collective-permute-done((bf16[384,384]{1,0:T(8,128)(2,1)}, bf16[384,384]{1,0:T(8,128)(2,1)S(1)}, u32[]{:S(2)}, u32[]{:S(2)}) %collective-permute-start.7) | collective-permute-done | bytes 294944 | tf_op jit(solution)/shard_map/ppermute | solution.py:527
  54.7 6.8 %collective-permute-start.14 = (bf16[512,512]{1,0:T(8,128)(2,1)S(1)}, bf16[512,512]{1,0:T(8,128)(2,1)S(1)}, u32[]{:S(2)}, u32[]{:S(2)}) collective-permute-start(bf16[512,512]{1,0:T(8,128)(2,1)S(1)} %collective-permute-done.9.refs_1_), channel_id=1, source_target_pairs={{0,8},{8,16},{16,24},{24,0},{1,9},{9,17},{17,25},{25,1},{2,10},{10... | collective-permute-start | bytes 1572872 | tf_op jit(solution)/shard_map/ppermute | solution.py:74
  63.2 9.5 %shard_map.119 = (bf16[384,128]{1,0:T(8,128)(2,1)}, bf16[384,128]{1,0:T(8,128)(2,1)}, bf16[384,128]{1,0:T(8,128)(2,1)}, bf16[384,128]{1,0:T(8,128)(2,1)}) custom-call(bf16[384,384]{1,0:T(8,128)(2,1)} %get-tuple-element.103.refs_0_, bf16[384,384]{1,0:T(8,128)(2,1)} %copy-done.14, bf16[384,384]{1,0:T(8,128)(2,1)} %copy-done.15, bf16[384,384]{1,0:T(8,128)(2,1)} %copy-done.16), custom_call_target="tpu_custom_call" | custom-call | tf_op jit(solution)/shard_map/pallas_call | solution.py:306
  76.4 19.0 %collective-permute-done.13.refs_1_ = bf16[256,512]{1,0:T(8,128)(2,1)} collective-permute-done((bf16[256,512]{1,0:T(8,128)(2,1)S(1)}, bf16[256,512]{1,0:T(8,128)(2,1)}, u32[]{:S(2)}, u32[]{:S(2)}) %collective-permute-start.13) | collective-permute-done | bytes 262176 | tf_op jit(solution)/shard_map/ppermute | solution.py:74
  95.4 8.2 %collective-permute-done.11.refs_2_ = bf16[384,128]{1,0:T(8,128)(2,1)S(1)} collective-permute-done((bf16[384,128]{1,0:T(8,128)(2,1)}, bf16[384,128]{1,0:T(8,128)(2,1)S(1)}, u32[]{:S(2)}, u32[]{:S(2)}) %collective-permute-start.11) | collective-permute-done | bytes 98336 | tf_op jit(solution)/shard_map/ppermute | solution.py:732
  112.0 16.4 %conditional.3 = (f32[96,2048]{1,0:T(8,128)S(1)}, bf16[96,2048]{1,0:T(8,128)(2,1)}) conditional(s32[]{:T(128)} %convert_element_type.54, () %tuple.47, (bf16[2,96,2048]{2,1,0:T(8,128)(2,1)}, f32[2,96,2048]{2,1,0:T(8,128)}) %shard_map.120), branch_computations={%region_0.0_spmd, %region_1.2_spmd} | conditional | flops 786468 | bytes 11010523 | solution.py:217
  118.6 9.8 %collective-permute-done.1 = bf16[1,96,2048]{2,1,0:T(8,128)(2,1)} collective-permute-done((bf16[1,96,2048]{2,1,0:T(8,128)(2,1)}, bf16[1,96,2048]{2,1,0:T(8,128)(2,1)}, u32[]{:S(2)}, u32[]{:S(2)}) %collective-permute-start.1) | collective-permute-done | bytes 393248 | tf_op jit(solution)/shard_map/cond/branch_1_fun/ppermute | solution.py:230
  128.4 5.7 %collective-permute-done.16.refs_3_ = bf16[256,512]{1,0:T(8,128)(2,1)} collective-permute-done((bf16[256,512]{1,0:T(8,128)(2,1)}, bf16[256,512]{1,0:T(8,128)(2,1)}, u32[]{:S(2)}, u32[]{:S(2)}) %collective-permute-start.16) | collective-permute-done | bytes 262176 | tf_op jit(solution)/shard_map/ppermute | solution.py:74
  134.2 5.8 %collective-permute-start.20 = (bf16[256,512]{1,0:T(8,128)(2,1)}, bf16[256,512]{1,0:T(8,128)(2,1)}, u32[]{:S(2)}, u32[]{:S(2)}) collective-permute-start(bf16[256,512]{1,0:T(8,128)(2,1)} %collective-permute-done.16.refs_3_), channel_id=1, source_target_pairs={{0,8},{8,16},{16,24},{24,0},{1,9},{9,17},{17,25},{25,1},{2,10},{10... | collective-permute-start | bytes 786440 | tf_op jit(solution)/shard_map/ppermute | solution.py:74
  142.2 10.7 %conditional.4 = (bf16[384,2048]{1,0:T(8,128)(2,1)S(1)}) conditional(s32[]{:T(128)} %convert_element_type.54, () %tuple.57, bf16[96,2048]{1,0:T(8,128)(2,1)S(1)} %get-tuple-element.137), branch_computations={%region_2.3_spmd, %region_3.4_spmd} | conditional | flops 2752547 | bytes 17301940 | solution.py:217
  143.7 6.3 %collective-permute-done.2 = bf16[1,96,2048]{2,1,0:T(8,128)(2,1)S(1)} collective-permute-done((bf16[1,96,2048]{2,1,0:T(8,128)(2,1)S(1)}, bf16[1,96,2048]{2,1,0:T(8,128)(2,1)S(1)}, u32[]{:S(2)}, u32[]{:S(2)}) %collective-permute-start.2) | collective-permute-done | bytes 393248 | tf_op jit(solution)/shard_map/cond/branch_1_fun/ppermute | solution.py:248
  156.0 5.9 %collective-permute-start.26 = (bf16[1024,128]{1,0:T(8,128)(2,1)S(1)}, bf16[1024,128]{1,0:T(8,128)(2,1)S(1)}, u32[]{:S(2)}, u32[]{:S(2)}) collective-permute-start(bf16[1024,128]{1,0:T(8,128)(2,1)S(1)} %dynamic-slice.28.refs_0_), channel_id=1, source_target_pairs={{0,8},{8,16},{16,24},{24,0},{1,9},{9,17},{17,25},{25,1},{2,10},{10... | collective-permute-start | bytes 786440 | tf_op jit(solution)/shard_map/ppermute | solution.py:74
  161.9 4.9 %shard_map.122.x_ref = bf16[384,512]{1,0:T(8,128)(2,1)} custom-call(bf16[384,2048]{1,0:T(8,128)(2,1)S(1)} %get-tuple-element.205.x_ref, bf16[512,512]{1,0:T(8,128)(2,1)} %refs_0_.2, bf16[512,512]{1,0:T(8,128)(2,1)} %copy-done.8, bf16[512,512]{1,0:T(8,128)(2,1)} %copy-done.10, bf16[512,512]{1,0:T(8,128)(2,1)} %copy-done.9, ...), custom_call_target="tpu_custom_call" | custom-call | tf_op jit(solution)/shard_map/pallas_call | solution.py:306
  178.5 9.3 %shard_map.123 = (bf16[2,96,2048]{2,1,0:T(8,128)(2,1)S(1)}, f32[2,96,2048]{2,1,0:T(8,128)}) custom-call(bf16[384,512]{1,0:T(8,128)(2,1)} %shard_map.122.x_ref, bf16[16,512]{1,0:T(8,128)(2,1)} %copy-done.26, bf16[16,512]{1,0:T(8,128)(2,1)} %copy-done.27, f32[31,512]{1,0:T(8,128)} %taps_ref.1, bf16[512,512]{1,0:T(8,128)(2,1)} %refs_0_.3, ...), custom_call_target="tpu_custom_call" | custom-call | tf_op jit(solution)/shard_map/pallas_call | solution.py:306
  187.8 15.3 %conditional.5 = (f32[96,2048]{1,0:T(8,128)S(1)}, bf16[96,2048]{1,0:T(8,128)(2,1)}) conditional(s32[]{:T(128)} %convert_element_type.54, () %tuple.56, (bf16[2,96,2048]{2,1,0:T(8,128)(2,1)S(1)}, f32[2,96,2048]{2,1,0:T(8,128)}) %shard_map.123), branch_computations={%region_4.5_spmd, %region_5.6_spmd} | conditional | flops 786468 | bytes 11010523 | solution.py:217
  193.4 9.7 %collective-permute-done.5 = bf16[1,96,2048]{2,1,0:T(8,128)(2,1)} collective-permute-done((bf16[1,96,2048]{2,1,0:T(8,128)(2,1)S(1)}, bf16[1,96,2048]{2,1,0:T(8,128)(2,1)}, u32[]{:S(2)}, u32[]{:S(2)}) %collective-permute-start.5) | collective-permute-done | bytes 393248 | tf_op jit(solution)/shard_map/cond/branch_1_fun/ppermute | solution.py:230
  203.1 5.1 %collective-permute-start.27 = (bf16[1024,128]{1,0:T(8,128)(2,1)S(1)}, bf16[1024,128]{1,0:T(8,128)(2,1)S(1)}, u32[]{:S(2)}, u32[]{:S(2)}) collective-permute-start(bf16[1024,128]{1,0:T(8,128)(2,1)S(1)} %collective-permute-done.26.refs_1_), channel_id=1, source_target_pairs={{0,8},{8,16},{16,24},{24,0},{1,9},{9,17},{17,25},{25,1},{2,10},{10... | collective-permute-start | bytes 786440 | tf_op jit(solution)/shard_map/ppermute | solution.py:74
  221.5 5.6 %collective-permute-done.30 = bf16[96,2048]{1,0:T(8,128)(2,1)S(1)} collective-permute-done((bf16[96,2048]{1,0:T(8,128)(2,1)}, bf16[96,2048]{1,0:T(8,128)(2,1)S(1)}, u32[]{:S(2)}, u32[]{:S(2)}) %collective-permute-start.30) | collective-permute-done | bytes 393248 | tf_op jit(solution)/shard_map/ppermute | solution.py:258
  240.2 8.9 %shard_map.125.left_ref = bf16[768,1024]{1,0:T(8,128)(2,1)} custom-call(f32[6,8]{1,0:T(8,128)} %constant_dynamic-slice_fusion.1.mask_ref, bf16[384,2048]{1,0:T(8,128)(2,1)} %copy-done.2, bf16[384,2048]{1,0:T(8,128)(2,1)} %copy-done.3, bf16[2048,1024]{1,0:T(8,128)(2,1)} %all-gather.6.cloned.1.call-done.refs_2_), custom_call_target="tpu_custom_call" | custom-call | tf_op jit(solution)/shard_map/pallas_call | solution.py:306
  252.5 4.7 %shard_map.126 = (bf16[2,2,96,512]{3,2,1,0:T(8,128)(2,1)}, f32[2,2,96,512]{3,2,1,0:T(8,128)}) custom-call(bf16[768,1024]{1,0:T(8,128)(2,1)} %shard_map.125.left_ref, bf16[1024,128]{1,0:T(8,128)(2,1)} %copy-done.7, bf16[1024,128]{1,0:T(8,128)(2,1)} %copy-done.17, bf16[1024,128]{1,0:T(8,128)(2,1)} %copy-done.19, bf16[1024,128]{1,0:T(8,128)(2,1)} %collective-permute-done.34.refs_3_), custom_call_target="tpu_custom_call" | custom-call | tf_op jit(solution)/shard_map/pallas_call | solution.py:306
  268.1 10.6 %all-gather.8.cloned.1.call-done.refs_0_ = bf16[4096,384]{1,0:T(8,128)(2,1)} async-done(((bf16[1024,384]{1,0:T(8,128)(2,1)}), bf16[4096,384]{1,0:T(8,128)(2,1)}) %all-gather.8.cloned.1.call-update) | async-done | bytes 3145744 | tf_op jit(solution)/shard_map/all_gather | solution.py:150
  278.7 8.6 %shard_map.127 = (bf16[2,2,96,1536]{3,2,1,0:T(8,128)(2,1)}, f32[2,2,96,1536]{3,2,1,0:T(8,128)}) custom-call(bf16[768,1024]{1,0:T(8,128)(2,1)} %shard_map.125.left_ref, bf16[4096,384]{1,0:T(8,128)(2,1)} %all-gather.8.cloned.1.call-done.refs_0_), custom_call_target="tpu_custom_call" | custom-call | tf_op jit(solution)/shard_map/pallas_call | solution.py:306
  302.8 4.9 %collective-permute-done.42.refs_1_ = bf16[96,1536]{1,0:T(8,128)(2,1)S(1)} collective-permute-done((bf16[96,1536]{1,0:T(8,128)(2,1)S(1)}, bf16[96,1536]{1,0:T(8,128)(2,1)S(1)}, u32[]{:S(2)}, u32[]{:S(2)}) %collective-permute-start.42) | collective-permute-done | bytes 294944 | tf_op jit(solution)/shard_map/ppermute | solution.py:258
  (194 shorter events, 123.5 us)
Async XLA Ops:
  6.5 100.8 %all-gather.4.cloned.1.call-start = ((), (), s32[]{:S(2)}) async-start(), calls=%async_computation | async-start | bytes 2359296 | tf_op jit(solution)/shard_map/all_gather | solution.py:150
  8.4 230.6 %all-gather.6.cloned.1.call-start = ((), (), s32[]{:S(2)}) async-start(), calls=%async_computation.1 | async-start | bytes 5242880 | tf_op jit(solution)/shard_map/all_gather | solution.py:150
  9.6 269.1 %all-gather.8.cloned.1.call-start = ((), (), s32[]{:S(2)}) async-start(), calls=%async_computation.2 | async-start | bytes 3932160 | tf_op jit(solution)/shard_map/all_gather | solution.py:150
  10.1 44.6 %collective-permute-start.9 = (bf16[512,512]{1,0:T(8,128)(2,1)S(1)}, bf16[512,512]{1,0:T(8,128)(2,1)S(1)}, u32[]{:S(2)}, u32[]{:S(2)}) collective-permute-start(bf16[512,512]{1,0:T(8,128)(2,1)S(1)} %pad_maximum_fusion.1), channel_id=1, source_target_pairs={{0,8},{8,16},{16,24},{24,0},{1,9},{9,17},{17,25},{25,1},{2,10},{10... | collective-permute-start | bytes 1572872 | tf_op jit(solution)/shard_map/ppermute | solution.py:74
  15.7 27.1 %collective-permute-start.6 = (bf16[384,384]{1,0:T(8,128)(2,1)}, bf16[384,384]{1,0:T(8,128)(2,1)S(1)}, u32[]{:S(2)}, u32[]{:S(2)}) collective-permute-start(bf16[384,384]{1,0:T(8,128)(2,1)} %get-tuple-element.99), channel_id=1, source_target_pairs={{0,8},{8,16},{16,24},{24,0},{1,9},{9,17},{17,25},{25,1},{2,10},{10... | collective-permute-start | bytes 884744 | tf_op jit(solution)/shard_map/ppermute | solution.py:527
  17.3 37.4 %collective-permute-start.7 = (bf16[384,384]{1,0:T(8,128)(2,1)}, bf16[384,384]{1,0:T(8,128)(2,1)S(1)}, u32[]{:S(2)}, u32[]{:S(2)}) collective-permute-start(bf16[384,384]{1,0:T(8,128)(2,1)} %get-tuple-element.100), channel_id=1, source_target_pairs={{0,16},{8,24},{16,0},{24,8},{1,17},{9,25},{17,1},{25,9},{2,18},{10... | collective-permute-start | bytes 884744 | tf_op jit(solution)/shard_map/ppermute | solution.py:527
  18.3 36.4 %collective-permute-start.8 = (bf16[384,384]{1,0:T(8,128)(2,1)}, bf16[384,384]{1,0:T(8,128)(2,1)S(1)}, u32[]{:S(2)}, u32[]{:S(2)}) collective-permute-start(bf16[384,384]{1,0:T(8,128)(2,1)} %get-tuple-element.101), channel_id=1, source_target_pairs={{0,24},{8,0},{16,8},{24,16},{1,25},{9,1},{17,9},{25,17},{2,26},{10... | collective-permute-start | bytes 884744 | tf_op jit(solution)/shard_map/ppermute | solution.py:527
  54.7 48.9 %collective-permute-start.14 = (bf16[512,512]{1,0:T(8,128)(2,1)S(1)}, bf16[512,512]{1,0:T(8,128)(2,1)S(1)}, u32[]{:S(2)}, u32[]{:S(2)}) collective-permute-start(bf16[512,512]{1,0:T(8,128)(2,1)S(1)} %collective-permute-done.9.refs_1_), channel_id=1, source_target_pairs={{0,8},{8,16},{16,24},{24,0},{1,9},{9,17},{17,25},{25,1},{2,10},{10... | collective-permute-start | bytes 1572872 | tf_op jit(solution)/shard_map/ppermute | solution.py:74
  61.5 42.1 %collective-permute-start.15 = (bf16[512,512]{1,0:T(8,128)(2,1)S(1)}, bf16[512,512]{1,0:T(8,128)(2,1)S(1)}, u32[]{:S(2)}, u32[]{:S(2)}) collective-permute-start(bf16[512,512]{1,0:T(8,128)(2,1)S(1)} %collective-permute-done.9.refs_1_), channel_id=1, source_target_pairs={{0,1},{1,0},{2,3},{3,2},{4,5},{5,4},{6,7},{7,6},{8,9},{9,8},{10,11... | collective-permute-start | bytes 1572872 | tf_op jit(solution)/shard_map/ppermute | solution.py:93
  63.1 32.3 %collective-permute-start.13 = (bf16[256,512]{1,0:T(8,128)(2,1)S(1)}, bf16[256,512]{1,0:T(8,128)(2,1)}, u32[]{:S(2)}, u32[]{:S(2)}) collective-permute-start(bf16[256,512]{1,0:T(8,128)(2,1)S(1)} %constant_dynamic-slice_fusion.4), channel_id=1, source_target_pairs={{0,8},{8,16},{16,24},{24,0},{1,9},{9,17},{17,25},{25,1},{2,10},{10... | collective-permute-start | bytes 786440 | tf_op jit(solution)/shard_map/ppermute | solution.py:74
  72.6 22.8 %collective-permute-start.10 = (bf16[384,128]{1,0:T(8,128)(2,1)}, bf16[384,128]{1,0:T(8,128)(2,1)S(1)}, u32[]{:S(2)}, u32[]{:S(2)}) collective-permute-start(bf16[384,128]{1,0:T(8,128)(2,1)} %get-tuple-element.108), channel_id=1, source_target_pairs={{0,24},{8,0},{16,8},{24,16},{1,25},{9,1},{17,9},{25,17},{2,26},{10... | collective-permute-start | bytes 294920 | tf_op jit(solution)/shard_map/ppermute | solution.py:732
  76.4 27.2 %collective-permute-start.11 = (bf16[384,128]{1,0:T(8,128)(2,1)}, bf16[384,128]{1,0:T(8,128)(2,1)S(1)}, u32[]{:S(2)}, u32[]{:S(2)}) collective-permute-start(bf16[384,128]{1,0:T(8,128)(2,1)} %get-tuple-element.109), channel_id=1, source_target_pairs={{0,16},{8,24},{16,0},{24,8},{1,17},{9,25},{17,1},{25,9},{2,18},{10... | collective-permute-start | bytes 294920 | tf_op jit(solution)/shard_map/ppermute | solution.py:732
  103.7 30.4 %collective-permute-start.18 = (bf16[512,512]{1,0:T(8,128)(2,1)S(1)}, bf16[512,512]{1,0:T(8,128)(2,1)S(1)}, u32[]{:S(2)}, u32[]{:S(2)}) collective-permute-start(bf16[512,512]{1,0:T(8,128)(2,1)S(1)} %collective-permute-done.14.refs_3_), channel_id=1, source_target_pairs={{0,8},{8,16},{16,24},{24,0},{1,9},{9,17},{17,25},{25,1},{2,10},{10... | collective-permute-start | bytes 1572872 | tf_op jit(solution)/shard_map/ppermute | solution.py:74
  103.7 30.4 %collective-permute-start.19 = (bf16[512,512]{1,0:T(8,128)(2,1)S(1)}, bf16[512,512]{1,0:T(8,128)(2,1)}, u32[]{:S(2)}, u32[]{:S(2)}) collective-permute-start(bf16[512,512]{1,0:T(8,128)(2,1)S(1)} %collective-permute-done.14.refs_3_), channel_id=1, source_target_pairs={{0,1},{1,0},{2,3},{3,2},{4,5},{5,4},{6,7},{7,6},{8,9},{9,8},{10,11... | collective-permute-start | bytes 1572872 | tf_op jit(solution)/shard_map/ppermute | solution.py:93
  105.1 29.0 %collective-permute-start.16 = (bf16[256,512]{1,0:T(8,128)(2,1)}, bf16[256,512]{1,0:T(8,128)(2,1)}, u32[]{:S(2)}, u32[]{:S(2)}) collective-permute-start(bf16[256,512]{1,0:T(8,128)(2,1)} %collective-permute-done.13.refs_1_), channel_id=1, source_target_pairs={{0,8},{8,16},{16,24},{24,0},{1,9},{9,17},{17,25},{25,1},{2,10},{10... | collective-permute-start | bytes 786440 | tf_op jit(solution)/shard_map/ppermute | solution.py:74
  106.9 27.2 %collective-permute-start.17 = (bf16[256,512]{1,0:T(8,128)(2,1)}, bf16[256,512]{1,0:T(8,128)(2,1)}, u32[]{:S(2)}, u32[]{:S(2)}) collective-permute-start(bf16[256,512]{1,0:T(8,128)(2,1)} %collective-permute-done.13.refs_1_), channel_id=1, source_target_pairs={{0,1},{1,0},{2,3},{3,2},{4,5},{5,4},{6,7},{7,6},{8,9},{9,8},{10,11... | collective-permute-start | bytes 786440 | tf_op jit(solution)/shard_map/ppermute | solution.py:93
  134.1 27.8 %collective-permute-start.22 = (bf16[512,512]{1,0:T(8,128)(2,1)S(1)}, bf16[512,512]{1,0:T(8,128)(2,1)}, u32[]{:S(2)}, u32[]{:S(2)}) collective-permute-start(bf16[512,512]{1,0:T(8,128)(2,1)S(1)} %collective-permute-done.18.refs_5_), channel_id=1, source_target_pairs={{0,1},{1,0},{2,3},{3,2},{4,5},{5,4},{6,7},{7,6},{8,9},{9,8},{10,11... | collective-permute-start | bytes 1572872 | tf_op jit(solution)/shard_map/ppermute | solution.py:93
  134.2 18.7 %collective-permute-start.20 = (bf16[256,512]{1,0:T(8,128)(2,1)}, bf16[256,512]{1,0:T(8,128)(2,1)}, u32[]{:S(2)}, u32[]{:S(2)}) collective-permute-start(bf16[256,512]{1,0:T(8,128)(2,1)} %collective-permute-done.16.refs_3_), channel_id=1, source_target_pairs={{0,8},{8,16},{16,24},{24,0},{1,9},{9,17},{17,25},{25,1},{2,10},{10... | collective-permute-start | bytes 786440 | tf_op jit(solution)/shard_map/ppermute | solution.py:74
  140.0 12.9 %collective-permute-start.21 = (bf16[256,512]{1,0:T(8,128)(2,1)}, bf16[256,512]{1,0:T(8,128)(2,1)S(1)}, u32[]{:S(2)}, u32[]{:S(2)}) collective-permute-start(bf16[256,512]{1,0:T(8,128)(2,1)} %collective-permute-done.16.refs_3_), channel_id=1, source_target_pairs={{0,1},{1,0},{2,3},{3,2},{4,5},{5,4},{6,7},{7,6},{8,9},{9,8},{10,11... | collective-permute-start | bytes 786440 | tf_op jit(solution)/shard_map/ppermute | solution.py:93
  153.0 20.3 %collective-permute-start.23 = (bf16[256,512]{1,0:T(8,128)(2,1)}, bf16[256,512]{1,0:T(8,128)(2,1)S(1)}, u32[]{:S(2)}, u32[]{:S(2)}) collective-permute-start(bf16[256,512]{1,0:T(8,128)(2,1)} %collective-permute-done.20.refs_5_), channel_id=1, source_target_pairs={{0,1},{1,0},{2,3},{3,2},{4,5},{5,4},{6,7},{7,6},{8,9},{9,8},{10,11... | collective-permute-start | bytes 786440 | tf_op jit(solution)/shard_map/ppermute | solution.py:93
  156.0 47.1 %collective-permute-start.26 = (bf16[1024,128]{1,0:T(8,128)(2,1)S(1)}, bf16[1024,128]{1,0:T(8,128)(2,1)S(1)}, u32[]{:S(2)}, u32[]{:S(2)}) collective-permute-start(bf16[1024,128]{1,0:T(8,128)(2,1)S(1)} %dynamic-slice.28.refs_0_), channel_id=1, source_target_pairs={{0,8},{8,16},{16,24},{24,0},{1,9},{9,17},{17,25},{25,1},{2,10},{10... | collective-permute-start | bytes 786440 | tf_op jit(solution)/shard_map/ppermute | solution.py:74
  236.1 16.4 %collective-permute-start.34 = (bf16[1024,128]{1,0:T(8,128)(2,1)S(1)}, bf16[1024,128]{1,0:T(8,128)(2,1)}, u32[]{:S(2)}, u32[]{:S(2)}) collective-permute-start(bf16[1024,128]{1,0:T(8,128)(2,1)S(1)} %collective-permute-done.27.refs_2_), channel_id=1, source_target_pairs={{0,8},{8,16},{16,24},{24,0},{1,9},{9,17},{17,25},{25,1},{2,10},{10... | collective-permute-start | bytes 786440 | tf_op jit(solution)/shard_map/ppermute | solution.py:74
  265.4 13.3 %collective-permute-start.37 = (bf16[96,512]{1,0:T(8,128)(2,1)S(1)}, bf16[96,512]{1,0:T(8,128)(2,1)S(1)}, u32[]{:S(2)}, u32[]{:S(2)}) collective-permute-start(bf16[96,512]{1,0:T(8,128)(2,1)S(1)} %pad_maximum_fusion.4), channel_id=1, source_target_pairs={{0,1},{1,0},{2,3},{3,2},{4,5},{5,4},{6,7},{7,6},{8,9},{9,8},{10,11... | collective-permute-start | bytes 294920 | tf_op jit(solution)/shard_map/ppermute | solution.py:258
  266.8 11.9 %collective-permute-start.39 = (bf16[96,512]{1,0:T(8,128)(2,1)S(1)}, bf16[96,512]{1,0:T(8,128)(2,1)S(1)}, u32[]{:S(2)}, u32[]{:S(2)}) collective-permute-start(bf16[96,512]{1,0:T(8,128)(2,1)S(1)} %pad_maximum_fusion.5), channel_id=1, source_target_pairs={{0,4},{2,6},{4,0},{6,2},{1,5},{3,7},{5,1},{7,3},{8,12},{10,14},{12... | collective-permute-start | bytes 294920 | tf_op jit(solution)/shard_map/ppermute | solution.py:258
  (53 other events, 444.9 us)
Sparse Core Ops, SparseCore 0:
  9.5 94.6 all-gather.3
  105.7 98.4 all-gather.5
  210.5 68.1 all-gather.7

commit v3 on v2

--- a/solution.py
+++ b/solution.py
@@ -755,7 +755,7 @@
     units = line.visits(0, units)
     units = line.until(["conv_out"], units)
     sent, kept = conv_branch(units, depth_kernel, line.take("conv_out"), before, after)
-    kept, taken = fenced(scatter_sum, sent, kept)
+    kept, taken = scatter_sum(sent, kept)
     kept, taken = line.visits(2, (kept, taken))
     stream, norm_two = advance(stream, kept, taken, False)
 

time: 319 us -> 317 us (level)
  starting transfers between devices: 71.6 us -> 62.8 us
  waiting for transfers between devices: 149 us -> 153 us
    ppermute x9, waiting for transfers between devices: 32.5 us -> 43 us  [refill(): lax.ppermute(piece, 'seq', ring_pairs('seq'))]
    ppermute x4, waiting for transfers between devices: 24.2 us -> 14.4 us  [scatter_sum(): taken = lax.ppermute(sent, 'mp', xor_pairs(count, bit))]
    ppermute x9, starting transfers between devices: 29.1 us -> 22.7 us  [refill(): lax.ppermute(piece, 'seq', ring_pairs('seq'))]
    ppermute x16, waiting for transfers between devices: 28.7 us -> 33.1 us  [swap(): return lax.ppermute(value, axis, xor_pairs(lax.axis_size(axis), bit))]
  transfers between devices with their start and end apart: 48 -> 48, of which waited for: 29 -> 28; matrix products, arithmetic and copies ran while one was open for 5% -> 5% of each run, Pallas kernels for 15% -> 16%
where the time goes in v3:
time: 317 us
  waiting for transfers between devices  153 us (48%)
  starting transfers between devices  62.8 us (20%)
  Pallas kernels  61.1 us (19%)
  local copies, waits for them, and re-layouts  18 us (6%)
  between operations  13.5 us (4%)
  other arithmetic  7.97 us (3%)
    pallas_call x11, Pallas kernels, kernel_call(): pl.pallas_call(kernel, out_shape=outs, in_specs=[pl.BlockSpec(memory_spac...  61.1 us
    ppermute x9, waiting for transfers between devices, refill(): lax.ppermute(piece, 'seq', ring_pairs('seq'))  43 us
    ppermute x16, waiting for transfers between devices, swap(): return lax.ppermute(value, axis, xor_pairs(lax.axis_size(axis), bit))  33.1 us
    ppermute x3, waiting for transfers between devices, heads_by_device(): lax.ppermute(pieces[d], 'seq', [(i, (i + d) % count) for i in range(count)])  31.7 us
    ppermute x9, starting transfers between devices, refill(): lax.ppermute(piece, 'seq', ring_pairs('seq'))  22.7 us
    ppermute x4, waiting for transfers between devices, scatter_sum(): taken = lax.ppermute(sent, 'mp', xor_pairs(count, bit))  14.4 us
    ppermute x16, starting transfers between devices, swap(): return lax.ppermute(value, axis, xor_pairs(lax.axis_size(axis), bit))  14.2 us
    ppermute x2, waiting for transfers between devices, widen(): taken = lax.ppermute(held, 'mp', xor_pairs(count, bit))  8.4 us
  transfers between devices with their start and end apart: 48, of which 28 were waited for; matrix products, arithmetic and copies ran while one was open for 5% of the time, Pallas kernels for 16%

profile of v3, /device:TPU:0, one launch (start us, length us, event | category | flops | bytes accessed | tf_op | source)
XLA Modules:
  0.0 316.6 jit_solution(11985312657449621045)
XLA Ops:
  23.0 19.8 %collective-permute-done.4.refs_1_ = bf16[384,384]{1,0:T(8,128)(2,1)S(1)} collective-permute-done((bf16[384,384]{1,0:T(8,128)(2,1)}, bf16[384,384]{1,0:T(8,128)(2,1)S(1)}, u32[]{:S(2)}, u32[]{:S(2)}) %collective-permute-start.4) | collective-permute-done | bytes 294944 | tf_op jit(solution)/shard_map/ppermute | solution.py:527
  42.8 11.9 %collective-permute-done.5.refs_2_ = bf16[384,384]{1,0:T(8,128)(2,1)S(1)} collective-permute-done((bf16[384,384]{1,0:T(8,128)(2,1)}, bf16[384,384]{1,0:T(8,128)(2,1)S(1)}, u32[]{:S(2)}, u32[]{:S(2)}) %collective-permute-start.5) | collective-permute-done | bytes 294944 | tf_op jit(solution)/shard_map/ppermute | solution.py:527
  54.7 6.8 %collective-permute-start.12 = (bf16[512,512]{1,0:T(8,128)(2,1)S(1)}, bf16[512,512]{1,0:T(8,128)(2,1)}, u32[]{:S(2)}, u32[]{:S(2)}) collective-permute-start(bf16[512,512]{1,0:T(8,128)(2,1)S(1)} %collective-permute-done.7.refs_1_), channel_id=1, source_target_pairs={{0,8},{8,16},{16,24},{24,0},{1,9},{9,17},{17,25},{25,1},{2,10},{10... | collective-permute-start | bytes 1572872 | tf_op jit(solution)/shard_map/ppermute | solution.py:74
  63.2 9.4 %shard_map.119 = (bf16[384,128]{1,0:T(8,128)(2,1)}, bf16[384,128]{1,0:T(8,128)(2,1)}, bf16[384,128]{1,0:T(8,128)(2,1)}, bf16[384,128]{1,0:T(8,128)(2,1)}) custom-call(bf16[384,384]{1,0:T(8,128)(2,1)} %get-tuple-element.97.refs_0_, bf16[384,384]{1,0:T(8,128)(2,1)} %copy-done.15, bf16[384,384]{1,0:T(8,128)(2,1)} %copy-done.16, bf16[384,384]{1,0:T(8,128)(2,1)} %copy-done.17), custom_call_target="tpu_custom_call" | custom-call | tf_op jit(solution)/shard_map/pallas_call | solution.py:306
  76.4 19.0 %collective-permute-done.11.refs_1_ = bf16[256,512]{1,0:T(8,128)(2,1)} collective-permute-done((bf16[256,512]{1,0:T(8,128)(2,1)S(1)}, bf16[256,512]{1,0:T(8,128)(2,1)}, u32[]{:S(2)}, u32[]{:S(2)}) %collective-permute-start.11) | collective-permute-done | bytes 262176 | tf_op jit(solution)/shard_map/ppermute | solution.py:74
  95.4 8.2 %collective-permute-done.9.refs_2_ = bf16[384,128]{1,0:T(8,128)(2,1)S(1)} collective-permute-done((bf16[384,128]{1,0:T(8,128)(2,1)}, bf16[384,128]{1,0:T(8,128)(2,1)S(1)}, u32[]{:S(2)}, u32[]{:S(2)}) %collective-permute-start.9) | collective-permute-done | bytes 98336 | tf_op jit(solution)/shard_map/ppermute | solution.py:732
  112.5 15.3 %conditional.2 = (f32[96,2048]{1,0:T(8,128)S(1)}, bf16[96,2048]{1,0:T(8,128)(2,1)}) conditional(s32[]{:T(128)} %convert_element_type.53, () %tuple.40, (bf16[2,96,2048]{2,1,0:T(8,128)(2,1)S(1)}, f32[2,96,2048]{2,1,0:T(8,128)}) %shard_map.120), branch_computations={%region_0.0_spmd, %region_1.2_spmd} | conditional | flops 786468 | bytes 11010523 | solution.py:217
  118.2 9.6 %collective-permute-done.1 = bf16[1,96,2048]{2,1,0:T(8,128)(2,1)} collective-permute-done((bf16[1,96,2048]{2,1,0:T(8,128)(2,1)S(1)}, bf16[1,96,2048]{2,1,0:T(8,128)(2,1)}, u32[]{:S(2)}, u32[]{:S(2)}) %collective-permute-start.1) | collective-permute-done | bytes 393248 | tf_op jit(solution)/shard_map/cond/branch_1_fun/ppermute | solution.py:230
  127.8 8.2 %collective-permute-done.14.refs_3_ = bf16[256,512]{1,0:T(8,128)(2,1)} collective-permute-done((bf16[256,512]{1,0:T(8,128)(2,1)}, bf16[256,512]{1,0:T(8,128)(2,1)}, u32[]{:S(2)}, u32[]{:S(2)}) %collective-permute-start.14) | collective-permute-done | bytes 262176 | tf_op jit(solution)/shard_map/ppermute | solution.py:74
  136.1 6.4 %collective-permute-start.18 = (bf16[256,512]{1,0:T(8,128)(2,1)}, bf16[256,512]{1,0:T(8,128)(2,1)}, u32[]{:S(2)}, u32[]{:S(2)}) collective-permute-start(bf16[256,512]{1,0:T(8,128)(2,1)} %collective-permute-done.14.refs_3_), channel_id=1, source_target_pairs={{0,8},{8,16},{16,24},{24,0},{1,9},{9,17},{17,25},{25,1},{2,10},{10... | collective-permute-start | bytes 786440 | tf_op jit(solution)/shard_map/ppermute | solution.py:74
  145.0 11.9 %conditional.3 = (bf16[384,2048]{1,0:T(8,128)(2,1)S(1)}) conditional(s32[]{:T(128)} %convert_element_type.53, () %tuple.49, bf16[96,2048]{1,0:T(8,128)(2,1)} %get-tuple-element.131), branch_computations={%region_2.3_spmd, %region_3.4_spmd} | conditional | flops 2752547 | bytes 17301940 | solution.py:217
  146.8 6.1 %collective-permute-done.2 = bf16[1,96,2048]{2,1,0:T(8,128)(2,1)S(1)} collective-permute-done((bf16[1,96,2048]{2,1,0:T(8,128)(2,1)}, bf16[1,96,2048]{2,1,0:T(8,128)(2,1)S(1)}, u32[]{:S(2)}, u32[]{:S(2)}) %collective-permute-start.2) | collective-permute-done | bytes 393248 | tf_op jit(solution)/shard_map/cond/branch_1_fun/ppermute | solution.py:248
  159.6 5.0 %shard_map.122.x_ref = bf16[384,512]{1,0:T(8,128)(2,1)} custom-call(bf16[384,2048]{1,0:T(8,128)(2,1)S(1)} %get-tuple-element.195.x_ref, bf16[512,512]{1,0:T(8,128)(2,1)} %refs_0_.2, bf16[512,512]{1,0:T(8,128)(2,1)} %copy-done.8, bf16[512,512]{1,0:T(8,128)(2,1)} %copy-done.9, bf16[512,512]{1,0:T(8,128)(2,1)} %collective-permute-done.12.refs_3_, ...), custom_call_target="tpu_custom_call" | custom-call | tf_op jit(solution)/shard_map/pallas_call | solution.py:306
  165.4 4.6 %collective-permute-start.22 = (bf16[16,512]{1,0:T(8,128)(2,1)S(1)}, bf16[16,512]{1,0:T(8,128)(2,1)S(1)}, u32[]{:S(2)}, u32[]{:S(2)}) collective-permute-start(bf16[16,512]{1,0:T(8,128)(2,1)S(1)} %get-tuple-element.182), channel_id=1, source_target_pairs={{0,8},{8,16},{16,24},{1,9},{9,17},{17,25},{2,10},{10,18},{18,26},{... | collective-permute-start | bytes 49160 | tf_op jit(solution)/shard_map/ppermute | solution.py:753
  171.5 5.9 %collective-permute-done.23.after_ref = bf16[16,512]{1,0:T(8,128)(2,1)S(1)} collective-permute-done((bf16[16,512]{1,0:T(8,128)(2,1)S(1)}, bf16[16,512]{1,0:T(8,128)(2,1)S(1)}, u32[]{:S(2)}, u32[]{:S(2)}) %collective-permute-start.23) | collective-permute-done | bytes 16416 | tf_op jit(solution)/shard_map/ppermute | solution.py:754
  178.0 9.6 %shard_map.123 = (bf16[2,96,2048]{2,1,0:T(8,128)(2,1)}, f32[2,96,2048]{2,1,0:T(8,128)}) custom-call(bf16[384,512]{1,0:T(8,128)(2,1)} %shard_map.122.x_ref, bf16[16,512]{1,0:T(8,128)(2,1)} %copy-done.27, bf16[16,512]{1,0:T(8,128)(2,1)} %copy-done.28, f32[31,512]{1,0:T(8,128)} %taps_ref.1, bf16[512,512]{1,0:T(8,128)(2,1)} %refs_0_.3, ...), custom_call_target="tpu_custom_call" | custom-call | tf_op jit(solution)/shard_map/pallas_call | solution.py:306
  198.5 6.6 %collective-permute-done.26.refs_1_ = bf16[1024,128]{1,0:T(8,128)(2,1)S(1)} collective-permute-done((bf16[1024,128]{1,0:T(8,128)(2,1)S(1)}, bf16[1024,128]{1,0:T(8,128)(2,1)S(1)}, u32[]{:S(2)}, u32[]{:S(2)}) %collective-permute-start.26) | collective-permute-done | bytes 262176 | tf_op jit(solution)/shard_map/ppermute | solution.py:74
  208.4 6.5 %collective-permute-done.27.refs_2_ = bf16[1024,128]{1,0:T(8,128)(2,1)S(1)} collective-permute-done((bf16[1024,128]{1,0:T(8,128)(2,1)S(1)}, bf16[1024,128]{1,0:T(8,128)(2,1)S(1)}, u32[]{:S(2)}, u32[]{:S(2)}) %collective-permute-start.27) | collective-permute-done | bytes 262176 | tf_op jit(solution)/shard_map/ppermute | solution.py:74
  220.4 7.4 %collective-permute-done.30 = bf16[96,2048]{1,0:T(8,128)(2,1)S(1)} collective-permute-done((bf16[96,2048]{1,0:T(8,128)(2,1)}, bf16[96,2048]{1,0:T(8,128)(2,1)S(1)}, u32[]{:S(2)}, u32[]{:S(2)}) %collective-permute-start.30) | collective-permute-done | bytes 393248 | tf_op jit(solution)/shard_map/ppermute | solution.py:258
  240.9 8.9 %shard_map.125.left_ref = bf16[768,1024]{1,0:T(8,128)(2,1)} custom-call(f32[6,8]{1,0:T(8,128)} %constant_dynamic-slice_fusion.1.mask_ref, bf16[384,2048]{1,0:T(8,128)(2,1)} %copy-done.2, bf16[384,2048]{1,0:T(8,128)(2,1)} %copy-done.3, bf16[2048,1024]{1,0:T(8,128)(2,1)} %all-gather.6.cloned.1.call-done.refs_2_), custom_call_target="tpu_custom_call" | custom-call | tf_op jit(solution)/shard_map/pallas_call | solution.py:306
  252.4 4.8 %shard_map.126 = (bf16[2,2,96,512]{3,2,1,0:T(8,128)(2,1)}, f32[2,2,96,512]{3,2,1,0:T(8,128)}) custom-call(bf16[768,1024]{1,0:T(8,128)(2,1)} %shard_map.125.left_ref, bf16[1024,128]{1,0:T(8,128)(2,1)} %copy-done.7, bf16[1024,128]{1,0:T(8,128)(2,1)} %copy-done.18, bf16[1024,128]{1,0:T(8,128)(2,1)} %copy-done.19, bf16[1024,128]{1,0:T(8,128)(2,1)} %collective-permute-done.34.refs_3_), custom_call_target="tpu_custom_call" | custom-call | tf_op jit(solution)/shard_map/pallas_call | solution.py:306
  269.0 8.1 %all-gather.8.cloned.1.call-done.refs_0_ = bf16[4096,384]{1,0:T(8,128)(2,1)} async-done(((bf16[1024,384]{1,0:T(8,128)(2,1)}), bf16[4096,384]{1,0:T(8,128)(2,1)}) %all-gather.8.cloned.1.call-update) | async-done | bytes 3145744 | tf_op jit(solution)/shard_map/all_gather | solution.py:150
  277.1 8.6 %shard_map.127 = (bf16[2,2,96,1536]{3,2,1,0:T(8,128)(2,1)}, f32[2,2,96,1536]{3,2,1,0:T(8,128)}) custom-call(bf16[768,1024]{1,0:T(8,128)(2,1)} %shard_map.125.left_ref, bf16[4096,384]{1,0:T(8,128)(2,1)} %all-gather.8.cloned.1.call-done.refs_0_), custom_call_target="tpu_custom_call" | custom-call | tf_op jit(solution)/shard_map/pallas_call | solution.py:306
  301.1 4.9 %collective-permute-done.42.refs_1_ = bf16[96,1536]{1,0:T(8,128)(2,1)S(1)} collective-permute-done((bf16[96,1536]{1,0:T(8,128)(2,1)S(1)}, bf16[96,1536]{1,0:T(8,128)(2,1)S(1)}, u32[]{:S(2)}, u32[]{:S(2)}) %collective-permute-start.42) | collective-permute-done | bytes 294944 | tf_op jit(solution)/shard_map/ppermute | solution.py:258
  (195 shorter events, 116.7 us)
Async XLA Ops:
  6.5 101.5 %all-gather.4.cloned.1.call-start = ((), (), s32[]{:S(2)}) async-start(), calls=%async_computation | async-start | bytes 2359296 | tf_op jit(solution)/shard_map/all_gather | solution.py:150
  8.4 231.3 %all-gather.6.cloned.1.call-start = ((), (), s32[]{:S(2)}) async-start(), calls=%async_computation.1 | async-start | bytes 5242880 | tf_op jit(solution)/shard_map/all_gather | solution.py:150
  9.5 267.5 %all-gather.8.cloned.1.call-start = ((), (), s32[]{:S(2)}) async-start(), calls=%async_computation.2 | async-start | bytes 3932160 | tf_op jit(solution)/shard_map/all_gather | solution.py:150
  10.1 44.6 %collective-permute-start.7 = (bf16[512,512]{1,0:T(8,128)(2,1)S(1)}, bf16[512,512]{1,0:T(8,128)(2,1)S(1)}, u32[]{:S(2)}, u32[]{:S(2)}) collective-permute-start(bf16[512,512]{1,0:T(8,128)(2,1)S(1)} %pad_maximum_fusion.1), channel_id=1, source_target_pairs={{0,8},{8,16},{16,24},{24,0},{1,9},{9,17},{17,25},{25,1},{2,10},{10... | collective-permute-start | bytes 1572872 | tf_op jit(solution)/shard_map/ppermute | solution.py:74
  15.7 27.2 %collective-permute-start.4 = (bf16[384,384]{1,0:T(8,128)(2,1)}, bf16[384,384]{1,0:T(8,128)(2,1)S(1)}, u32[]{:S(2)}, u32[]{:S(2)}) collective-permute-start(bf16[384,384]{1,0:T(8,128)(2,1)} %get-tuple-element.93), channel_id=1, source_target_pairs={{0,8},{8,16},{16,24},{24,0},{1,9},{9,17},{17,25},{25,1},{2,10},{10... | collective-permute-start | bytes 884744 | tf_op jit(solution)/shard_map/ppermute | solution.py:527
  17.2 37.4 %collective-permute-start.5 = (bf16[384,384]{1,0:T(8,128)(2,1)}, bf16[384,384]{1,0:T(8,128)(2,1)S(1)}, u32[]{:S(2)}, u32[]{:S(2)}) collective-permute-start(bf16[384,384]{1,0:T(8,128)(2,1)} %get-tuple-element.94), channel_id=1, source_target_pairs={{0,16},{8,24},{16,0},{24,8},{1,17},{9,25},{17,1},{25,9},{2,18},{10... | collective-permute-start | bytes 884744 | tf_op jit(solution)/shard_map/ppermute | solution.py:527
  18.3 36.4 %collective-permute-start.6 = (bf16[384,384]{1,0:T(8,128)(2,1)}, bf16[384,384]{1,0:T(8,128)(2,1)S(1)}, u32[]{:S(2)}, u32[]{:S(2)}) collective-permute-start(bf16[384,384]{1,0:T(8,128)(2,1)} %get-tuple-element.95), channel_id=1, source_target_pairs={{0,24},{8,0},{16,8},{24,16},{1,25},{9,1},{17,9},{25,17},{2,26},{10... | collective-permute-start | bytes 884744 | tf_op jit(solution)/shard_map/ppermute | solution.py:527
  54.7 48.9 %collective-permute-start.12 = (bf16[512,512]{1,0:T(8,128)(2,1)S(1)}, bf16[512,512]{1,0:T(8,128)(2,1)}, u32[]{:S(2)}, u32[]{:S(2)}) collective-permute-start(bf16[512,512]{1,0:T(8,128)(2,1)S(1)} %collective-permute-done.7.refs_1_), channel_id=1, source_target_pairs={{0,8},{8,16},{16,24},{24,0},{1,9},{9,17},{17,25},{25,1},{2,10},{10... | collective-permute-start | bytes 1572872 | tf_op jit(solution)/shard_map/ppermute | solution.py:74
  61.5 42.1 %collective-permute-start.13 = (bf16[512,512]{1,0:T(8,128)(2,1)S(1)}, bf16[512,512]{1,0:T(8,128)(2,1)S(1)}, u32[]{:S(2)}, u32[]{:S(2)}) collective-permute-start(bf16[512,512]{1,0:T(8,128)(2,1)S(1)} %collective-permute-done.7.refs_1_), channel_id=1, source_target_pairs={{0,1},{1,0},{2,3},{3,2},{4,5},{5,4},{6,7},{7,6},{8,9},{9,8},{10,11... | collective-permute-start | bytes 1572872 | tf_op jit(solution)/shard_map/ppermute | solution.py:93
  63.0 32.3 %collective-permute-start.11 = (bf16[256,512]{1,0:T(8,128)(2,1)S(1)}, bf16[256,512]{1,0:T(8,128)(2,1)}, u32[]{:S(2)}, u32[]{:S(2)}) collective-permute-start(bf16[256,512]{1,0:T(8,128)(2,1)S(1)} %constant_dynamic-slice_fusion.4), channel_id=1, source_target_pairs={{0,8},{8,16},{16,24},{24,0},{1,9},{9,17},{17,25},{25,1},{2,10},{10... | collective-permute-start | bytes 786440 | tf_op jit(solution)/shard_map/ppermute | solution.py:74
  72.6 22.8 %collective-permute-start.8 = (bf16[384,128]{1,0:T(8,128)(2,1)}, bf16[384,128]{1,0:T(8,128)(2,1)S(1)}, u32[]{:S(2)}, u32[]{:S(2)}) collective-permute-start(bf16[384,128]{1,0:T(8,128)(2,1)} %get-tuple-element.102), channel_id=1, source_target_pairs={{0,24},{8,0},{16,8},{24,16},{1,25},{9,1},{17,9},{25,17},{2,26},{10... | collective-permute-start | bytes 294920 | tf_op jit(solution)/shard_map/ppermute | solution.py:732
  76.4 27.2 %collective-permute-start.9 = (bf16[384,128]{1,0:T(8,128)(2,1)}, bf16[384,128]{1,0:T(8,128)(2,1)S(1)}, u32[]{:S(2)}, u32[]{:S(2)}) collective-permute-start(bf16[384,128]{1,0:T(8,128)(2,1)} %get-tuple-element.103), channel_id=1, source_target_pairs={{0,16},{8,24},{16,0},{24,8},{1,17},{9,25},{17,1},{25,9},{2,18},{10... | collective-permute-start | bytes 294920 | tf_op jit(solution)/shard_map/ppermute | solution.py:732
  104.5 31.6 %collective-permute-start.16 = (bf16[512,512]{1,0:T(8,128)(2,1)}, bf16[512,512]{1,0:T(8,128)(2,1)S(1)}, u32[]{:S(2)}, u32[]{:S(2)}) collective-permute-start(bf16[512,512]{1,0:T(8,128)(2,1)} %collective-permute-done.12.refs_3_), channel_id=1, source_target_pairs={{0,8},{8,16},{16,24},{24,0},{1,9},{9,17},{17,25},{25,1},{2,10},{10... | collective-permute-start | bytes 1572872 | tf_op jit(solution)/shard_map/ppermute | solution.py:74
  104.5 31.6 %collective-permute-start.17 = (bf16[512,512]{1,0:T(8,128)(2,1)}, bf16[512,512]{1,0:T(8,128)(2,1)}, u32[]{:S(2)}, u32[]{:S(2)}) collective-permute-start(bf16[512,512]{1,0:T(8,128)(2,1)} %collective-permute-done.12.refs_3_), channel_id=1, source_target_pairs={{0,1},{1,0},{2,3},{3,2},{4,5},{5,4},{6,7},{7,6},{8,9},{9,8},{10,11... | collective-permute-start | bytes 1572872 | tf_op jit(solution)/shard_map/ppermute | solution.py:93
  105.8 30.3 %collective-permute-start.14 = (bf16[256,512]{1,0:T(8,128)(2,1)}, bf16[256,512]{1,0:T(8,128)(2,1)}, u32[]{:S(2)}, u32[]{:S(2)}) collective-permute-start(bf16[256,512]{1,0:T(8,128)(2,1)} %collective-permute-done.11.refs_1_), channel_id=1, source_target_pairs={{0,8},{8,16},{16,24},{24,0},{1,9},{9,17},{17,25},{25,1},{2,10},{10... | collective-permute-start | bytes 786440 | tf_op jit(solution)/shard_map/ppermute | solution.py:74
  107.6 28.4 %collective-permute-start.15 = (bf16[256,512]{1,0:T(8,128)(2,1)}, bf16[256,512]{1,0:T(8,128)(2,1)}, u32[]{:S(2)}, u32[]{:S(2)}) collective-permute-start(bf16[256,512]{1,0:T(8,128)(2,1)} %collective-permute-done.11.refs_1_), channel_id=1, source_target_pairs={{0,1},{1,0},{2,3},{3,2},{4,5},{5,4},{6,7},{7,6},{8,9},{9,8},{10,11... | collective-permute-start | bytes 786440 | tf_op jit(solution)/shard_map/ppermute | solution.py:93
  116.5 11.3 %collective-permute-start.1 = (bf16[1,96,2048]{2,1,0:T(8,128)(2,1)S(1)}, bf16[1,96,2048]{2,1,0:T(8,128)(2,1)}, u32[]{:S(2)}, u32[]{:S(2)}) collective-permute-start(bf16[1,96,2048]{2,1,0:T(8,128)(2,1)S(1)} %dynamic-slice_convert_fusion), channel_id=1, source_target_pairs={{0,4},{2,6},{4,0},{6,2},{1,5},{3,7},{5,1},{7,3},{8,12},{10,14},{12... | collective-permute-start | bytes 1179656 | tf_op jit(solution)/shard_map/cond/branch_1_fun/ppermute | solution.py:230
  136.0 22.8 %collective-permute-start.20 = (bf16[512,512]{1,0:T(8,128)(2,1)S(1)}, bf16[512,512]{1,0:T(8,128)(2,1)S(1)}, u32[]{:S(2)}, u32[]{:S(2)}) collective-permute-start(bf16[512,512]{1,0:T(8,128)(2,1)S(1)} %collective-permute-done.16.refs_5_), channel_id=1, source_target_pairs={{0,1},{1,0},{2,3},{3,2},{4,5},{5,4},{6,7},{7,6},{8,9},{9,8},{10,11... | collective-permute-start | bytes 1572872 | tf_op jit(solution)/shard_map/ppermute | solution.py:93
  136.1 20.7 %collective-permute-start.18 = (bf16[256,512]{1,0:T(8,128)(2,1)}, bf16[256,512]{1,0:T(8,128)(2,1)}, u32[]{:S(2)}, u32[]{:S(2)}) collective-permute-start(bf16[256,512]{1,0:T(8,128)(2,1)} %collective-permute-done.14.refs_3_), channel_id=1, source_target_pairs={{0,8},{8,16},{16,24},{24,0},{1,9},{9,17},{17,25},{25,1},{2,10},{10... | collective-permute-start | bytes 786440 | tf_op jit(solution)/shard_map/ppermute | solution.py:74
  142.5 14.4 %collective-permute-start.19 = (bf16[256,512]{1,0:T(8,128)(2,1)}, bf16[256,512]{1,0:T(8,128)(2,1)}, u32[]{:S(2)}, u32[]{:S(2)}) collective-permute-start(bf16[256,512]{1,0:T(8,128)(2,1)} %collective-permute-done.14.refs_3_), channel_id=1, source_target_pairs={{0,1},{1,0},{2,3},{3,2},{4,5},{5,4},{6,7},{7,6},{8,9},{9,8},{10,11... | collective-permute-start | bytes 786440 | tf_op jit(solution)/shard_map/ppermute | solution.py:93
  156.9 14.4 %collective-permute-start.21 = (bf16[256,512]{1,0:T(8,128)(2,1)}, bf16[256,512]{1,0:T(8,128)(2,1)S(1)}, u32[]{:S(2)}, u32[]{:S(2)}) collective-permute-start(bf16[256,512]{1,0:T(8,128)(2,1)} %collective-permute-done.18.refs_5_), channel_id=1, source_target_pairs={{0,1},{1,0},{2,3},{3,2},{4,5},{5,4},{6,7},{7,6},{8,9},{9,8},{10,11... | collective-permute-start | bytes 786440 | tf_op jit(solution)/shard_map/ppermute | solution.py:93
  191.7 13.4 %collective-permute-start.25 = (bf16[1,96,2048]{2,1,0:T(8,128)(2,1)S(1)}, bf16[1,96,2048]{2,1,0:T(8,128)(2,1)S(1)}, u32[]{:S(2)}, u32[]{:S(2)}) collective-permute-start(bf16[1,96,2048]{2,1,0:T(8,128)(2,1)S(1)} %dynamic-slice_convert_fusion.1), channel_id=1, source_target_pairs={{0,4},{2,6},{4,0},{6,2},{1,5},{3,7},{5,1},{7,3},{8,12},{10,14},{12... | collective-permute-start | bytes 1179656 | tf_op jit(solution)/shard_map/ppermute | solution.py:230
  217.9 11.5 %collective-permute-start.29 = (bf16[96,2048]{1,0:T(8,128)(2,1)}, bf16[96,2048]{1,0:T(8,128)(2,1)S(1)}, u32[]{:S(2)}, u32[]{:S(2)}) collective-permute-start(bf16[96,2048]{1,0:T(8,128)(2,1)} %get-tuple-element.155), channel_id=1, source_target_pairs={{0,4},{2,6},{4,0},{6,2},{1,5},{3,7},{5,1},{7,3},{8,12},{10,14},{12... | collective-permute-start | bytes 1179656 | tf_op jit(solution)/shard_map/ppermute | solution.py:258
  236.0 16.4 %collective-permute-start.34 = (bf16[1024,128]{1,0:T(8,128)(2,1)S(1)}, bf16[1024,128]{1,0:T(8,128)(2,1)}, u32[]{:S(2)}, u32[]{:S(2)}) collective-permute-start(bf16[1024,128]{1,0:T(8,128)(2,1)S(1)} %copy-done.20), channel_id=1, source_target_pairs={{0,8},{8,16},{16,24},{24,0},{1,9},{9,17},{17,25},{25,1},{2,10},{10... | collective-permute-start | bytes 786440 | tf_op jit(solution)/shard_map/ppermute | solution.py:74
  (54 other events, 445.6 us)
Sparse Core Ops, SparseCore 0:
  9.5 94.5 all-gather.3
  105.6 94.3 all-gather.5
  208.5 68.4 all-gather.7
